TPU v7x, 256 devices: a whole 4x4x8 slice. The times are simulated.
256 devices in a mesh: dp: 32 (over y, z_hi, core), tensor: 8 (over x, z_lo).
Axes of the slice: x: 4, y: 4, z: 8 (z_hi: 4, z_lo: 2; z = z_hi * 2 + z_lo), core: 2. Of those that a mesh axis runs over, the one named last changes fastest.
Arguments:
- layer_inputs: bfloat16 [32, 384, 16384], P(None, 'tensor', 'dp'), may hold values from -6 to 6
- out_grads: bfloat16 [16384, 28672], P('dp', 'tensor'), may hold values from -4 to 4
- projector: float32 [12288, 256], P(('dp', 'tensor')), may hold values from -2 to 2
- weights: bfloat16 [12288, 28672], P('dp', 'tensor'), may hold values from -6 to 6
- moment_first: float32 [256, 28672], P('dp', 'tensor'), may hold values from -6 to 6
- moment_second: float32 [256, 28672], P('dp', 'tensor'), may hold values from 0.01 to 1
Outputs:
- new_weights: bfloat16 [12288, 28672], P('dp', 'tensor')
- new_first: float32 [256, 28672], P('dp', 'tensor')
- new_second: float32 [256, 28672], P('dp', 'tensor')
- increment: float32 [12288, 256], P(('dp', 'tensor'))
All inputs are finite; a program needn't handle non-finite values.
Results may differ from a plain program's by a relative error of at most 0.019.
Values may be sent and summed in bfloat16 or wider, within the bound.
No kernel may reach another device: no remote copies, remote signals or barrier semaphores. Data moves between devices by JAX's collectives and lax.ppermute only.
A program may use at most 64 MiB of HBM per device.

v0:
```python
import jax
import jax.numpy as jnp
from jax import lax
from jax.sharding import PartitionSpec as P

beta_first = 0.9
beta_second = 0.999
bias_first = 1.0 / (1.0 - 0.9**10)
bias_second = 1.0 / (1.0 - 0.999**10)
epsilon = 1e-08
weight_rate = 2.0
proj_rate = 0.0002


def adam_rows(gradient, first, second):
    new_first = beta_first * first + (1.0 - beta_first) * gradient
    new_second = beta_second * second + (1.0 - beta_second) * gradient * gradient
    update = new_first * bias_first / (jnp.sqrt(new_second * bias_second) + epsilon)
    return (new_first, new_second, update.astype(jnp.bfloat16))


def increment_rows(feature_sum, proj_rows, gram_q, gram_k):
    highest = lax.Precision.HIGHEST
    first_term = jnp.dot(feature_sum, gram_q, precision=highest)
    second_term = jnp.dot(proj_rows, gram_k, precision=highest)
    return proj_rate * (4.0 * feature_sum - 2.0 * first_term - 2.0 * second_term)


def body(layer_inputs, out_grads, projector, weights, moment_first, moment_second):
    blocks, block_width, tokens_here = layer_inputs.shape
    flat_inputs = layer_inputs.reshape(blocks * block_width, tokens_here)
    rank_cols = projector.shape[1]
    own_rows = rank_cols // lax.axis_size("dp")
    proj_half = projector.astype(jnp.bfloat16)
    contract_rows = (((0,), (0,)), ((), ()))
    contract_cols = (((1,), (1,)), ((), ()))
    gram_own = lax.dot_general(
        proj_half, proj_half, contract_rows, preferred_element_type=jnp.float32
    )
    gram_q = lax.psum(gram_own, ("dp", "tensor"))
    inputs_rows = flat_inputs
    latent_part = lax.dot_general(
        inputs_rows,
        lax.all_gather(proj_half, "dp", axis=0, tiled=True),
        contract_rows,
        preferred_element_type=jnp.float32,
    )
    latent_sum = lax.psum(latent_part, "tensor")
    latent = latent_sum.astype(jnp.bfloat16)
    proj_block = lax.all_gather(proj_half, "tensor", axis=0, tiled=True)
    grad_local = lax.dot_general(
        latent, out_grads, contract_rows, preferred_element_type=jnp.float32
    )
    gradient = lax.psum(grad_local, "dp")
    grad_half = gradient.astype(jnp.bfloat16)
    grad_own = lax.dynamic_slice_in_dim(gradient, lax.axis_index("dp") * own_rows, own_rows, 0)
    new_first, new_second, update = adam_rows(grad_own, moment_first, moment_second)
    change = jnp.dot(
        proj_block,
        lax.all_gather(update, "dp", axis=0, tiled=True),
        preferred_element_type=jnp.float32,
    )
    new_weights = (weights.astype(jnp.float32) - weight_rate * change).astype(jnp.bfloat16)
    token_part = lax.dot_general(
        out_grads, grad_half, contract_cols, preferred_element_type=jnp.float32
    )
    gram_k_part = lax.dot_general(
        grad_half, grad_half, contract_cols, preferred_element_type=jnp.float32
    )
    token_rank, gram_k = lax.psum((token_part, gram_k_part), "tensor")
    token_half = token_rank.astype(jnp.bfloat16)
    inputs_rows = flat_inputs
    feature_sum = lax.psum_scatter(
        jnp.dot(inputs_rows, token_half, preferred_element_type=jnp.float32).astype(jnp.bfloat16),
        "dp",
        scatter_dimension=0,
        tiled=True,
    ).astype(jnp.float32)
    increment = increment_rows(feature_sum, projector, gram_q, gram_k)
    return (new_weights, new_first, new_second, increment)


def solution(mesh):
    placed = (
        P(None, "tensor", "dp"),
        P("dp", "tensor"),
        P(("dp", "tensor"), None),
        P("dp", "tensor"),
        P("dp", "tensor"),
        P("dp", "tensor"),
    )
    return jax.shard_map(
        body,
        mesh=mesh,
        in_specs=placed,
        out_specs=(
            P("dp", "tensor"),
            P("dp", "tensor"),
            P("dp", "tensor"),
            P(("dp", "tensor"), None),
        ),
        check_vma=False,
    )
```

profile of v0, /device:TPU:1, one launch (start us, length us, event | category | flops | bytes accessed | tf_op | source)
XLA Modules:
  0.0 894.4 jit_solution(11975029552653007620)
XLA Ops:
  7.2 0.0 copy-start
  7.2 0.0 all-reduce.6.cloned.1.call-start
  7.2 0.9 convert_element_type.31
  8.1 51.2 %all_gather.9 = bf16[1536,256]{1,0:T(8,128)(2,1)S(1)} all-gather(bf16[48,256]{1,0:T(8,128)(2,1)S(1)} %convert_element_type.31), channel_id=1, replica_groups=mesh['dp'=32,'tensor'=8] {'dp'}, dimensions={0}, use_global_device_ids=true | all-gather | bytes 811008 | tf_op jit(solution)/shard_map/all_gather | solution.py:44
  59.3 0.0 copy-done
  59.3 0.6 fusion.16
  59.9 37.3 %all-reduce.11 = bf16[512,256]{1,0:T(8,128)(2,1)S(1)} all-reduce(f32[512,256]{1,0:T(8,128)S(1)} %fusion.16), channel_id=1, replica_groups=mesh['dp'=32,'tensor'=8] {'tensor'}, use_global_device_ids=true, to_apply=%region_0.0 | all-reduce | flops 131072 | bytes 786432 | tf_op jit(solution)/shard_map/psum | solution.py:48
  97.3 5.0 fusion.18
  102.3 0.0 all-reduce.6.cloned.1.call-update
  102.3 0.0 all-reduce.10.cloned.1.call-start
  102.4 293.6 %all-reduce.6.cloned.1.call-done = f32[256,3584]{1,0:T(8,128)} async-done(((f32[256,3584]{1,0:T(8,128)}), f32[256,3584]{1,0:T(8,128)}) %all-reduce.6.cloned.1.call-update) | async-done | bytes 3670032 | tf_op jit(solution)/shard_map/psum | solution.py:54
  396.0 4.5 fusion.8
  400.6 0.0 all-reduce.10.cloned.1.call-update
  400.6 0.0 all-reduce.8.cloned.1.call-start
  400.6 0.9 fusion.17
  401.5 0.0 all-reduce.8.cloned.1.call-update
  401.6 0.0 reduce-scatter.4.cloned.1.call-start
  401.6 4.3 convolution_bitcast_fusion
  405.9 0.0 copy-start.2
  405.9 0.0 copy-start.3
  405.9 40.2 %all-reduce.12 = bf16[512,256]{0,1:T(8,128)(2,1)S(1)} all-reduce(f32[512,256]{0,1:T(8,128)S(1)} %convolution_bitcast_fusion), channel_id=1, replica_groups=mesh['dp'=32,'tensor'=8] {'tensor'}, use_global_device_ids=true, to_apply=%region_2.0 | all-reduce | flops 131072 | bytes 786432 | tf_op jit(solution)/shard_map/psum | solution.py:70
  446.2 0.6 fusion.3
  446.8 1.2 copy.18
  447.9 0.0 reduce-scatter.4.cloned.1.call-update
  448.0 0.0 all-gather.2.cloned.1.call-start
  448.0 0.0 copy-done.2
  448.0 0.0 copy-done.3
  448.0 1.7 divide_convert_fusion
  449.7 0.0 all-gather.2.cloned.1.call-update
  449.7 0.0 copy-start.1
  449.7 4.5 copy.15
  454.2 24.5 %all_gather.11 = bf16[384,256]{1,0:T(8,128)(2,1)S(1)} all-gather(bf16[48,256]{1,0:T(8,128)(2,1)S(1)} %convert_element_type.31), channel_id=1, replica_groups=mesh['dp'=32,'tensor'=8] {'tensor'}, dimensions={0}, use_global_device_ids=true | all-gather | bytes 221184 | tf_op jit(solution)/shard_map/all_gather | solution.py:50
  478.7 0.0 all-reduce.10.cloned.1.call-done
  478.7 0.0 copy-done.1
  478.7 1.2 fusion.4
  479.9 251.9 %all-reduce.8.cloned.1.call-done = f32[256,256]{1,0:T(8,128)} async-done(((f32[256,256]{1,0:T(8,128)}), f32[256,256]{1,0:T(8,128)}) %all-reduce.8.cloned.1.call-update) | async-done | bytes 262160 | tf_op jit(solution)/shard_map/psum | solution.py:40
  731.8 90.6 %reduce-scatter.4.cloned.1.call-done = bf16[48,256]{1,0:T(8,128)(2,1)} async-done(((bf16[1536,256]{1,0:T(8,128)(2,1)}), bf16[48,256]{1,0:T(8,128)(2,1)}) %reduce-scatter.4.cloned.1.call-update) | async-done | bytes 24592
  822.4 1.8 fusion.7
  824.2 54.1 %all-gather.2.cloned.1.call-done = bf16[256,3584]{1,0:T(8,128)(2,1)} async-done(((bf16[8,3584]{1,0:T(8,128)(2,1)}), bf16[256,3584]{1,0:T(8,128)(2,1)}) %all-gather.2.cloned.1.call-update) | async-done | bytes 1835024 | tf_op jit(solution)/shard_map/all_gather | solution.py:60
  878.4 5.1 fusion.2
  883.4 4.5 copy.17
Async XLA Ops:
  7.2 52.2 %copy-start = (bf16[32,48,512]{2,1,0:T(8,128)(2,1)S(1)}, bf16[32,48,512]{2,1,0:T(8,128)(2,1)}, u32[]{:S(2)}) copy-start(bf16[32,48,512]{2,1,0:T(8,128)(2,1)} %param.6) | copy-start | bytes 4718596
  7.2 388.8 %all-reduce.6.cloned.1.call-start = ((), (), s32[]{:S(2)}) async-start(), calls=%async_computation.1 | async-start | bytes 7340032 | tf_op jit(solution)/shard_map/psum | solution.py:54
  102.3 376.4 %all-reduce.10.cloned.1.call-start = ((), (), s32[]{:S(2)}) async-start(), calls=%async_computation.4 | async-start | bytes 524288 | tf_op jit(solution)/shard_map/psum | solution.py:70
  400.6 331.3 %all-reduce.8.cloned.1.call-start = ((), (), s32[]{:S(2)}) async-start(), calls=%async_computation.3 | async-start | bytes 524288 | tf_op jit(solution)/shard_map/psum | solution.py:40
  401.6 420.9 %reduce-scatter.4.cloned.1.call-start = ((), (), s32[]{:S(2)}) async-start(), calls=%async_computation.5 | async-start | bytes 811008
  405.9 42.1 %copy-start.2 = (f32[8,3584]{1,0:T(8,128)S(1)}, f32[8,3584]{1,0:T(8,128)}, u32[]{:S(2)}) copy-start(f32[8,3584]{1,0:T(8,128)} %param.10) | copy-start | bytes 344068
  405.9 42.1 %copy-start.3 = (f32[8,3584]{1,0:T(8,128)S(1)}, f32[8,3584]{1,0:T(8,128)}, u32[]{:S(2)}) copy-start(f32[8,3584]{1,0:T(8,128)} %param.11) | copy-start | bytes 344068
  448.0 430.4 %all-gather.2.cloned.1.call-start = ((), (), s32[]{:S(2)}) async-start(), calls=%async_computation.2 | async-start | bytes 1892352 | tf_op jit(solution)/shard_map/all_gather | solution.py:60
  449.7 29.0 %copy-start.1 = (f32[48,256]{1,0:T(8,128)S(1)}, f32[48,256]{1,0:T(8,128)}, u32[]{:S(2)}) copy-start(f32[48,256]{1,0:T(8,128)} %param.8) | copy-start | bytes 147460
Sparse Core Ops, SparseCore 0:
  102.5 293.4 all-reduce.5
  400.7 72.6 all-reduce.9
  478.9 252.8 all-reduce.7
  735.5 86.9 reduce-scatter.3
  824.8 53.4 all-gather.1
where the time goes:
time: 895 us; the launch traced here: 894 us
  waiting for transfers between devices  690 us (77%)
  blocking collectives  153 us (17%)
  matrix products  24 us (3%)
  between operations  13.9 us (2%)
  local copies, waits for them, and re-layouts  10.2 us (1%)
    psum x1, waiting for transfers between devices, body(): gradient = lax.psum(grad_local, 'dp')  294 us
    psum x1, waiting for transfers between devices, body(): gram_q = lax.psum(gram_own, ('dp', 'tensor'))  252 us
    unnamed x6, waiting for transfers between devices  90.7 us
    all_gather x1, waiting for transfers between devices, body(): lax.all_gather(update, 'dp', axis=0, tiled=True)  54.1 us
    all_gather x1, blocking collectives, body(): lax.all_gather(proj_half, 'dp', axis=0, tiled=True)  51.2 us
    psum x1, blocking collectives, body(): token_rank, gram_k = lax.psum((token_part, gram_k_part), 'tensor')  40.2 us
    psum x1, blocking collectives, body(): latent_sum = lax.psum(latent_part, 'tensor')  37.3 us
    all_gather x1, blocking collectives, body(): proj_block = lax.all_gather(proj_half, 'tensor', axis=0, tiled=True)  24.5 us
  transfers between devices with their start and end apart: 5, of which 4 were waited for; matrix products, arithmetic and copies ran while one was open for 2% of the time, Pallas kernels for 0%

commit v1 on v0

v1 whole, which is shorter than its diff:
```python
import jax
import jax.numpy as jnp
from jax import lax
from jax.experimental import pallas as pl
from jax.experimental.pallas import tpu as pltpu
from jax.sharding import PartitionSpec as P

beta_first = 0.9
beta_second = 0.999
bias_first = 1.0 / (1.0 - 0.9**10)
bias_second = 1.0 / (1.0 - 0.999**10)
epsilon = 1e-08
weight_rate = 2.0
proj_rate = 0.0002

bf16 = jnp.bfloat16
f32 = jnp.float32
HIGHEST = lax.Precision.HIGHEST
NY, NZ, NC = 4, 4, 2
NX, NL = 4, 2
TN = (((0,), (0,)), ((), ()))
NT = (((1,), (1,)), ((), ()))
MIB = 1024 * 1024


def dp_pairs(dy, dz, dc):
    return [
        (
            (y * NZ + z) * NC + c,
            (((y + dy) % NY) * NZ + (z + dz) % NZ) * NC + (c + dc) % NC,
        )
        for y in range(NY)
        for z in range(NZ)
        for c in range(NC)
    ]


def send_y(block, k):
    return lax.ppermute(block, "dp", dp_pairs(k, 0, 0))


def send_z(block, k):
    return lax.ppermute(block, "dp", dp_pairs(0, k, 0))


def send_core(block):
    return lax.ppermute(block, "dp", dp_pairs(0, 0, 1))


def send_xor(block, bit):
    return lax.ppermute(block, "tensor", [(j, j ^ bit) for j in range(NX * NL)])


def ring_blocks(block, send):
    got = {k: send(block, k) for k in (1, 3, 2)}
    return jnp.concatenate([block, got[3], got[2], got[1]], axis=0), got[1]


def gather_ring(block, send):
    return ring_blocks(block, send)[0]


def after(value, trigger):
    return lax.optimization_barrier((value, trigger))[0]


def split_high(value):
    high = value.astype(bf16)
    return high, (value - high.astype(f32)).astype(bf16)


def side_step(gram, rows, mask, trigger):
    n = gram.shape[0]
    eye = jnp.eye(n, dtype=f32)
    high, low = split_high(gram)
    rest = jnp.sum(low.astype(f32) * eye, axis=0).astype(bf16)
    payload = jnp.concatenate([high, jnp.broadcast_to(rest, (16, n)), rows], axis=0)
    got = send_xor(after(payload, trigger), mask)
    gram = gram + got[:n].astype(f32) + eye * got[n : n + 1].astype(f32)
    return gram, jnp.concatenate([rows, got[n + 16 :]], axis=0)


def split_sum(part):
    n = NX * NL
    rows, cols = part.shape
    got = lax.all_to_all(part.astype(bf16).reshape(n, rows // n, cols), "tensor", 0, 0)
    return jnp.sum(got.astype(f32), axis=0).astype(bf16)


def spread(own, extra=None):
    n = NX * NL
    rows, cols = own.shape
    blocks = jnp.broadcast_to(own, (n, rows, cols))
    if extra is not None:
        extra_rows = extra.shape[1]
        extra = jnp.pad(extra, ((0, 0), (0, rows - extra_rows), (0, 0)))
        blocks = jnp.concatenate([blocks, extra], axis=1)
    got = lax.all_to_all(blocks, "tensor", 0, 0)
    whole = got[:, :rows].reshape(n * rows, cols)
    return whole if extra is None else (whole, got[:, rows : rows + extra_rows])


def reduce_blocks(rows, send, beside=None):
    n = rows.shape[0] // 4
    got = [send(rows[k * n : (k + 1) * n].astype(bf16), k) for k in (1, 3, 2)]
    total = rows[:n].astype(f32)
    if beside is not None:
        total = after(total, beside)
    for block in got:
        total = total + block.astype(f32)
    return total, got[0]


def reduce_ring(rows, send):
    return reduce_blocks(rows, send)[0]


def one_hot(left, right):
    return (left[:, None] == right[None, :]).astype(bf16)


def turn_kernel(pos, x_ref, out_ref):
    z = pos[1]
    n = x_ref.shape[3]
    for k in range(NZ):
        out_ref[pl.ds(k * n, n), :] = x_ref[0, lax.rem(z + k, NZ), 0]


def turn_blocks(pos, x_view):
    block_width, tokens = x_view.shape[3:]
    rows = NZ * block_width
    return pl.pallas_call(
        turn_kernel,
        grid_spec=pltpu.PrefetchScalarGridSpec(
            num_scalar_prefetch=1,
            grid=(NC * NY,),
            in_specs=[
                pl.BlockSpec(
                    (1, NZ, 1, block_width, tokens),
                    lambda g, pos: (
                        lax.rem(pos[0] + lax.rem(g, NY), NY),
                        0,
                        lax.rem(pos[2] + lax.div(g, NY), NC),
                        0,
                        0,
                    ),
                ),
            ],
            out_specs=pl.BlockSpec((rows, tokens), lambda g, pos: (g, 0)),
        ),
        out_shape=jax.ShapeDtypeStruct((NC * NY * rows, tokens), bf16),
        compiler_params=pltpu.CompilerParams(vmem_limit_bytes=24 * MIB),
        cost_estimate=pl.CostEstimate(flops=0, bytes_accessed=12000000, transcendentals=0),
        name="turn",
    )(pos, x_view)


def gradient_kernel(latent_ref, cot_ref, keep_ref, send_ref):
    half = keep_ref.shape[0]
    for at in range(0, cot_ref.shape[1], 512):
        cols = pl.ds(at, 512)
        part = jnp.dot(latent_ref[...], cot_ref[:, cols], preferred_element_type=f32)
        keep_ref[:, cols] = part[:half]
        send_ref[:, cols] = part[half:].astype(bf16)


def gradient_parts(latent, out_grads):
    ranks, tokens = latent.shape
    cols = out_grads.shape[1]
    half = ranks // 2
    local = pl.BlockSpec(memory_space=pltpu.VMEM)
    return pl.pallas_call(
        gradient_kernel,
        in_specs=[local, local],
        out_specs=[local, local],
        out_shape=[
            jax.ShapeDtypeStruct((half, cols), f32),
            jax.ShapeDtypeStruct((half, cols), bf16),
        ],
        compiler_params=pltpu.CompilerParams(vmem_limit_bytes=24 * MIB),
        cost_estimate=pl.CostEstimate(
            flops=2 * ranks * tokens * cols, bytes_accessed=6500000, transcendentals=0
        ),
        name="gradient",
    )(latent, out_grads)


def weights_kernel(proj_ref, update_ref, weights_ref, out_ref):
    change = jnp.dot(proj_ref[...], update_ref[...], preferred_element_type=f32)
    out_ref[...] = (weights_ref[...].astype(f32) - weight_rate * change).astype(bf16)


def weights_step(proj_block, update, weights):
    rows, cols = weights.shape
    ranks = proj_block.shape[1]
    width = cols // 4
    return pl.pallas_call(
        weights_kernel,
        grid=(4,),
        in_specs=[
            pl.BlockSpec((rows, ranks), lambda g: (0, 0)),
            pl.BlockSpec((ranks, width), lambda g: (0, g)),
            pl.BlockSpec((rows, width), lambda g: (0, g)),
        ],
        out_specs=pl.BlockSpec((rows, width), lambda g: (0, g)),
        out_shape=jax.ShapeDtypeStruct((rows, cols), bf16),
        compiler_params=pltpu.CompilerParams(vmem_limit_bytes=56 * MIB),
        cost_estimate=pl.CostEstimate(
            flops=2 * rows * cols * ranks, bytes_accessed=8000000, transcendentals=0
        ),
        name="weights",
    )(proj_block, update, weights)


def adam_rows(gradient, first, second):
    new_first = beta_first * first + (1.0 - beta_first) * gradient
    new_second = beta_second * second + (1.0 - beta_second) * gradient * gradient
    update = new_first * bias_first / (jnp.sqrt(new_second * bias_second) + epsilon)
    return (new_first, new_second, update.astype(bf16))


def body(layer_inputs, out_grads, projector, weights, moment_first, moment_second):
    blocks, block_width, tokens = layer_inputs.shape
    ranks = projector.shape[1]
    dp = lax.axis_index("dp")
    tensor = lax.axis_index("tensor")
    y, z, c = dp // (NZ * NC), (dp // NC) % NZ, dp % NC
    pos = jnp.stack([y, z, c]).astype(jnp.int32)

    rank = jnp.arange(ranks, dtype=jnp.int32)
    rank_p = (
        ((rank // 32 + y) % NY) * 64
        + ((rank // 8 + z) % NZ) * 16
        + ((rank // 128 + c) % NC) * 8
        + rank % 8
    )
    p_from_r = one_hot(rank_p, rank)

    proj_half = projector.astype(bf16)
    quarter = gather_ring(proj_half, send_z)
    x_rel = turn_blocks(pos, layer_inputs.reshape(NY, NZ, NC, block_width, tokens))
    quarter, x_rel = lax.optimization_barrier((quarter, x_rel))
    proj_rel = gather_ring(quarter, send_y)
    proj_rel = jnp.concatenate([proj_rel, send_core(proj_rel)], axis=0)

    latent_own = split_sum(lax.dot_general(proj_rel, x_rel, TN, preferred_element_type=f32))
    gram_part = lax.dot_general(proj_rel, proj_rel, TN, preferred_element_type=f32)
    latent = spread(latent_own)
    latent_p = jnp.dot(p_from_r, latent, preferred_element_type=f32).astype(bf16)

    grad_keep, grad_send = gradient_parts(latent_p, out_grads)
    total = grad_keep + send_core(grad_send).astype(f32)
    total, first_got = reduce_blocks(total, send_y)
    side = side_step(gram_part, proj_half, 1, first_got)
    total, *side = lax.optimization_barrier((total, *side))
    gradient, first_got = reduce_blocks(total, send_z)
    side = side_step(*side, 2, first_got)
    grad_half = gradient.astype(bf16)
    new_first, new_second, update = adam_rows(gradient, moment_first, moment_second)
    grad_own, first_got = ring_blocks(grad_half, send_z)
    grad_own, *side = lax.optimization_barrier((grad_own, *side))
    update_all = lax.all_gather(update, "dp", axis=0, tiled=True)
    grad_own, first_got = ring_blocks(grad_own, send_y)
    side = side_step(*side, 6, first_got)
    grad_own, gram_q, proj_rows = lax.optimization_barrier((grad_own, *side))
    grad_p = jnp.concatenate([grad_own, send_core(grad_own)], axis=0)
    place = jnp.arange(8 * projector.shape[0], dtype=jnp.int32)
    block = place // block_width
    place_q = (block ^ ((block & 4) >> 1) ^ tensor) * block_width + place % block_width
    proj_block = jnp.dot(
        one_hot(place, place_q), proj_rows, preferred_element_type=f32
    ).astype(bf16)
    proj_block_p = lax.dot_general(
        proj_block, p_from_r, NT, preferred_element_type=f32
    ).astype(bf16)

    token_own = split_sum(lax.dot_general(grad_p, out_grads, NT, preferred_element_type=f32))
    gram_k = lax.dot_general(grad_p, grad_p, NT, preferred_element_type=f32).astype(bf16)
    second_part = jnp.dot(proj_block_p, gram_k, preferred_element_type=f32).astype(bf16)
    token_p, second = spread(token_own, second_part.reshape(NX * NL, -1, tokens))
    mix = 4.0 * jnp.eye(ranks, dtype=f32) - 2.0 * gram_q
    mix_p = jnp.concatenate(
        [
            jnp.dot(p_from_r, part, preferred_element_type=f32).astype(bf16)
            for part in split_high(mix)
        ],
        axis=0,
    )
    token_r = lax.dot_general(
        mix_p, jnp.concatenate([token_p, token_p], axis=0), TN, preferred_element_type=f32
    ).astype(bf16)

    n = x_rel.shape[0] // 2
    feat_send = lax.dot_general(x_rel[n:], token_r, NT, preferred_element_type=f32)
    feat_keep = lax.dot_general(x_rel[:n], token_r, NT, preferred_element_type=f32)
    total = feat_keep + send_core(feat_send.astype(bf16)).astype(f32)
    total = reduce_ring(total, send_y)
    new_weights = weights_step(proj_block, update_all, weights)
    feature_sum = reduce_blocks(total, send_z, new_weights)[0]

    second = jnp.sum(second.astype(f32), axis=0).reshape(block_width, ranks)
    second = jnp.dot(second, p_from_r.astype(f32), precision=HIGHEST)
    increment = proj_rate * (feature_sum - 2.0 * second)
    return (new_weights, new_first, new_second, increment)


def solution(mesh):
    placed = (
        P(None, "tensor", "dp"),
        P("dp", "tensor"),
        P(("dp", "tensor"), None),
        P("dp", "tensor"),
        P("dp", "tensor"),
        P("dp", "tensor"),
    )
    return jax.shard_map(
        body,
        mesh=mesh,
        in_specs=placed,
        out_specs=(
            P("dp", "tensor"),
            P("dp", "tensor"),
            P("dp", "tensor"),
            P(("dp", "tensor"), None),
        ),
        check_vma=False,
    )
```

time: 895 us -> 194 us (0.22)
  waiting for transfers between devices: 690 us -> 65.7 us
  blocking collectives: 153 us -> 11 us
  starting transfers between devices: 0.21 us -> 73.2 us
  matrix products: 24 us -> 10.3 us
    psum x3 -> x0, waiting for transfers between devices: 546 us -> none  [the longest x1 294 us: body(): gradient = lax.psum(grad_local, 'dp')]
    unnamed x6 -> x1, waiting for transfers between devices: 90.7 us -> 0.02 us
    psum x2 -> x0, blocking collectives: 77.6 us -> none  [the longest x1 40.2 us: body(): token_rank, gram_k = lax.psum((token_part, gram_k_part), 'tensor')]
    all_gather x2 -> x0, blocking collectives: 75.7 us -> none  [the longest x1 51.2 us: body(): lax.all_gather(proj_half, 'dp', axis=0, tiled=True)]
    ppermute x0 -> x31, starting transfers between devices: none -> 62.8 us  [the longest x12 32.6 us: send_z(): return lax.ppermute(block, 'dp', dp_pairs(0, k, 0))]
    all_gather x1, waiting for transfers between devices: 54.1 us -> 0.01 us  [body(): update_all = lax.all_gather(update, 'dp', axis=0, tiled=True)]
    ppermute x0 -> x31, waiting for transfers between devices: none -> 46.8 us  [the longest x12 27.5 us: send_y(): return lax.ppermute(block, 'dp', dp_pairs(k, 0, 0))]
    all_to_all x0 -> x3, waiting for transfers between devices: none -> 18.8 us  [the longest x2 14.7 us: spread(): got = lax.all_to_all(blocks, 'tensor', 0, 0)]
  transfers between devices with their start and end apart: 5 -> 35, of which waited for: 4 -> 23; matrix products, arithmetic and copies ran while one was open for 2% -> 6% of each run, Pallas kernels for 0% -> 3%
where the time goes in v1:
time: 194 us; the launch traced here: 192 us
  starting transfers between devices  73.2 us (38%)
  waiting for transfers between devices  65.7 us (34%)
  between operations  14.5 us (7%)
  blocking collectives  11 us (6%)
  matrix products  10.3 us (5%)
  Pallas kernels  7.34 us (4%)
  other arithmetic  5.5 us (3%)
  local copies, waits for them, and re-layouts  4.62 us (2%)
    ppermute x12, starting transfers between devices, send_z(): return lax.ppermute(block, 'dp', dp_pairs(0, k, 0))  32.6 us
    ppermute x12, waiting for transfers between devices, send_y(): return lax.ppermute(block, 'dp', dp_pairs(k, 0, 0))  27.5 us
    ppermute x4, starting transfers between devices, send_core(): return lax.ppermute(block, 'dp', dp_pairs(0, 0, 1))  16.7 us
    all_to_all x2, waiting for transfers between devices, spread(): got = lax.all_to_all(blocks, 'tensor', 0, 0)  14.7 us
    ppermute x12, starting transfers between devices, send_y(): return lax.ppermute(block, 'dp', dp_pairs(k, 0, 0))  12.2 us
    all_to_all x1, blocking collectives, split_sum(): lax.all_to_all(part.astype(bf16).reshape(n, rows // n, cols), 'tensor', 0...  11 us
    ppermute x12, waiting for transfers between devices, send_z(): return lax.ppermute(block, 'dp', dp_pairs(0, k, 0))  8.22 us
    all_to_all x2, starting transfers between devices, spread(): got = lax.all_to_all(blocks, 'tensor', 0, 0)  6.91 us
  transfers between devices with their start and end apart: 35, of which 23 were waited for; matrix products, arithmetic and copies ran while one was open for 6% of the time, Pallas kernels for 3%

profile of v1, /device:TPU:1, one launch (start us, length us, event | category | flops | bytes accessed | tf_op | source)
XLA Modules:
  0.0 192.1 jit_solution(10256433077751633331)
XLA Ops:
  8.0 6.8 %collective-permute-start = (bf16[48,256]{1,0:T(8,128)(2,1)S(1)}, bf16[48,256]{1,0:T(8,128)(2,1)S(1)}, u32[]{:S(2)}, u32[]{:S(2)}) collective-permute-start(bf16[48,256]{1,0:T(8,128)(2,1)S(1)} %convert_element_type.178), channel_id=1, source_target_pairs={{0,48},{8,56},{16,0},{24,8},{32,16},{40,24},{48,32},{56,40},{64,11... | collective-permute-start | bytes 73736 | tf_op jit(solution)/shard_map/ppermute | solution.py:43
  15.7 2.4 %collective-permute-start.2 = (bf16[48,256]{1,0:T(8,128)(2,1)S(1)}, bf16[48,256]{1,0:T(8,128)(2,1)S(1)}, u32[]{:S(2)}, u32[]{:S(2)}) collective-permute-start(bf16[48,256]{1,0:T(8,128)(2,1)S(1)} %convert_element_type.178), channel_id=1, source_target_pairs={{0,16},{8,24},{16,32},{24,40},{32,48},{40,56},{48,0},{56,8},{64,80... | collective-permute-start | bytes 73736 | tf_op jit(solution)/shard_map/ppermute | solution.py:43
  18.2 1.4 copy-done.2
  19.6 1.2 turn.1
  21.4 2.8 %collective-permute-start.3 = (bf16[192,256]{1,0:T(8,128)(2,1)S(1)}, bf16[192,256]{1,0:T(8,128)(2,1)S(1)}, u32[]{:S(2)}, u32[]{:S(2)}) collective-permute-start(bf16[192,256]{1,0:T(8,128)(2,1)S(1)} %pad_maximum_fusion.7), channel_id=1, source_target_pairs={{0,192},{8,200},{16,208},{24,216},{32,224},{40,232},{48,240},{56,2... | collective-permute-start | bytes 294920 | tf_op jit(solution)/shard_map/ppermute | solution.py:39
  25.9 3.4 %collective-permute-done.4 = bf16[192,256]{1,0:T(8,128)(2,1)S(1)} collective-permute-done((bf16[192,256]{1,0:T(8,128)(2,1)S(1)}, bf16[192,256]{1,0:T(8,128)(2,1)S(1)}, u32[]{:S(2)}, u32[]{:S(2)}) %collective-permute-start.4) | collective-permute-done | bytes 98336 | tf_op jit(solution)/shard_map/ppermute | solution.py:39
  30.3 3.6 %collective-permute-start.6 = (bf16[768,256]{1,0:T(8,128)(2,1)S(1)}, bf16[768,256]{1,0:T(8,128)(2,1)S(1)}, u32[]{:S(2)}, u32[]{:S(2)}) collective-permute-start(bf16[768,256]{1,0:T(8,128)(2,1)S(1)} %pad_maximum_fusion.1), channel_id=1, source_target_pairs={{0,8},{8,0},{16,24},{24,16},{32,40},{40,32},{48,56},{56,48},{64,72... | collective-permute-start | bytes 1179656 | tf_op jit(solution)/shard_map/ppermute | solution.py:47
  34.0 1.3 collective-permute-done.6
  35.9 11.0 %all_to_all.20 = bf16[8,32,512]{2,1,0:T(8,128)(2,1)S(1)} all-to-all(bf16[8,32,512]{2,1,0:T(8,128)(2,1)S(1)} %bitcast.27), channel_id=1, replica_groups=mesh['dp'=32,'tensor'=8] {'tensor'}, dimensions={0} | all-to-all | bytes 524288 | tf_op jit(solution)/shard_map/all_to_all | solution.py:86
  47.6 3.4 %all-to-all-start.1 = ((bf16[8,32,512]{2,1,0:T(8,128)(2,1)}), bf16[8,32,512]{2,1,0:T(8,128)(2,1)S(1)}, u32[]{:S(2)}, u32[]{:S(2)}) async-start(bf16[8,32,512]{2,1,0:T(8,128)(2,1)} %broadcast_in_dim.19), calls=%async_computation.1 | async-start | bytes 524288 | tf_op jit(solution)/shard_map/all_to_all | solution.py:98
  51.1 6.0 %all-to-all-done.1 = bf16[8,32,512]{2,1,0:T(8,128)(2,1)S(1)} async-done(((bf16[8,32,512]{2,1,0:T(8,128)(2,1)}), bf16[8,32,512]{2,1,0:T(8,128)(2,1)S(1)}, u32[]{:S(2)}, u32[]{:S(2)}) %all-to-all-start.1) | async-done | bytes 262176 | tf_op jit(solution)/shard_map/all_to_all | solution.py:98
  57.4 2.0 %copy-done = bf16[512,3584]{1,0:T(8,128)(2,1)S(1)} copy-done((bf16[512,3584]{1,0:T(8,128)(2,1)S(1)}, bf16[512,3584]{1,0:T(8,128)(2,1)}, u32[]{:S(2)}) %copy-start) | copy-done | bytes 3670040
  59.5 1.1 gradient.1
  60.6 2.7 %collective-permute-start.7 = (bf16[128,3584]{1,0:T(8,128)(2,1)S(1)}, bf16[128,3584]{1,0:T(8,128)(2,1)S(1)}, u32[]{:S(2)}, u32[]{:S(2)}) collective-permute-start(bf16[128,3584]{1,0:T(8,128)(2,1)S(1)} %get-tuple-element.24), channel_id=1, source_target_pairs={{0,8},{8,0},{16,24},{24,16},{32,40},{40,32},{48,56},{56,48},{64,72... | collective-permute-start | bytes 2752520 | tf_op jit(solution)/shard_map/ppermute | solution.py:47
  63.3 2.1 %collective-permute-done.7 = bf16[128,3584]{1,0:T(8,128)(2,1)S(1)} collective-permute-done((bf16[128,3584]{1,0:T(8,128)(2,1)S(1)}, bf16[128,3584]{1,0:T(8,128)(2,1)S(1)}, u32[]{:S(2)}, u32[]{:S(2)}) %collective-permute-start.7) | collective-permute-done | bytes 917536 | tf_op jit(solution)/shard_map/ppermute | solution.py:47
  65.8 1.5 collective-permute-start.10
  67.3 1.3 collective-permute-start.9
  69.0 9.7 %collective-permute-done.8 = bf16[32,3584]{1,0:T(8,128)(2,1)S(1)} collective-permute-done((bf16[32,3584]{1,0:T(8,128)(2,1)S(1)}, bf16[32,3584]{1,0:T(8,128)(2,1)S(1)}, u32[]{:S(2)}, u32[]{:S(2)}) %collective-permute-start.8) | collective-permute-done | bytes 229408 | tf_op jit(solution)/shard_map/ppermute | solution.py:39
  79.5 3.8 %collective-permute-done.11 = bf16[320,256]{1,0:T(8,128)(2,1)S(1)} collective-permute-done((bf16[320,256]{1,0:T(8,128)(2,1)S(1)}, bf16[320,256]{1,0:T(8,128)(2,1)S(1)}, u32[]{:S(2)}, u32[]{:S(2)}) %collective-permute-start.11) | collective-permute-done | bytes 163872 | tf_op jit(solution)/shard_map/ppermute | solution.py:51
  83.4 1.3 collective-permute-start.12
  84.6 2.4 %collective-permute-start.13 = (bf16[8,3584]{1,0:T(8,128)(2,1)S(1)}, bf16[8,3584]{1,0:T(8,128)(2,1)S(1)}, u32[]{:S(2)}, u32[]{:S(2)}) collective-permute-start(bf16[8,3584]{1,0:T(8,128)(2,1)S(1)} %get-tuple-element.60), channel_id=1, source_target_pairs={{0,48},{8,56},{16,0},{24,8},{32,16},{40,24},{48,32},{56,40},{64,11... | collective-permute-start | bytes 172040 | tf_op jit(solution)/shard_map/ppermute | solution.py:43
  87.0 3.9 %collective-permute-start.14 = (bf16[8,3584]{1,0:T(8,128)(2,1)S(1)}, bf16[8,3584]{1,0:T(8,128)(2,1)S(1)}, u32[]{:S(2)}, u32[]{:S(2)}) collective-permute-start(bf16[8,3584]{1,0:T(8,128)(2,1)S(1)} %get-tuple-element.59), channel_id=1, source_target_pairs={{0,32},{8,40},{16,48},{24,56},{32,0},{40,8},{48,16},{56,24},{64,96... | collective-permute-start | bytes 172040 | tf_op jit(solution)/shard_map/ppermute | solution.py:43
  90.9 4.2 %collective-permute-done.14 = bf16[8,3584]{1,0:T(8,128)(2,1)S(1)} collective-permute-done((bf16[8,3584]{1,0:T(8,128)(2,1)S(1)}, bf16[8,3584]{1,0:T(8,128)(2,1)S(1)}, u32[]{:S(2)}, u32[]{:S(2)}) %collective-permute-start.14) | collective-permute-done | bytes 57376 | tf_op jit(solution)/shard_map/ppermute | solution.py:43
  96.1 3.0 %collective-permute-start.16 = (bf16[8,3584]{1,0:T(8,128)(2,1)S(1)}, bf16[8,3584]{1,0:T(8,128)(2,1)S(1)}, u32[]{:S(2)}, u32[]{:S(2)}) collective-permute-start(bf16[8,3584]{1,0:T(8,128)(2,1)S(1)} %get-tuple-element.43), channel_id=1, source_target_pairs={{0,32},{8,40},{16,48},{24,56},{32,0},{40,8},{48,16},{56,24},{64,96... | collective-permute-start | bytes 172040 | tf_op jit(solution)/shard_map/ppermute | solution.py:43
  99.0 2.4 %collective-permute-start.17 = (bf16[8,3584]{1,0:T(8,128)(2,1)S(1)}, bf16[8,3584]{1,0:T(8,128)(2,1)S(1)}, u32[]{:S(2)}, u32[]{:S(2)}) collective-permute-start(bf16[8,3584]{1,0:T(8,128)(2,1)S(1)} %get-tuple-element.43), channel_id=1, source_target_pairs={{0,16},{8,24},{16,32},{24,40},{32,48},{40,56},{48,0},{56,8},{64,80... | collective-permute-start | bytes 172040 | tf_op jit(solution)/shard_map/ppermute | solution.py:43
  101.5 1.5 collective-permute-done.16
  103.0 1.8 collective-permute-done.17
  106.1 2.7 %collective-permute-start.19 = (bf16[32,3584]{1,0:T(8,128)(2,1)S(1)}, bf16[32,3584]{1,0:T(8,128)(2,1)S(1)}, u32[]{:S(2)}, u32[]{:S(2)}) collective-permute-start(bf16[32,3584]{1,0:T(8,128)(2,1)S(1)} %pad_maximum_fusion.3), channel_id=1, source_target_pairs={{0,192},{8,200},{16,208},{24,216},{32,224},{40,232},{48,240},{56,2... | collective-permute-start | bytes 688136 | tf_op jit(solution)/shard_map/ppermute | solution.py:39
  108.8 3.3 %collective-permute-done.21 = bf16[32,3584]{1,0:T(8,128)(2,1)S(1)} collective-permute-done((bf16[32,3584]{1,0:T(8,128)(2,1)S(1)}, bf16[32,3584]{1,0:T(8,128)(2,1)S(1)}, u32[]{:S(2)}, u32[]{:S(2)}) %collective-permute-start.21) | collective-permute-done | bytes 229408 | tf_op jit(solution)/shard_map/ppermute | solution.py:39
  112.7 1.5 collective-permute-done.19
  114.2 2.8 %collective-permute-done.20 = bf16[32,3584]{1,0:T(8,128)(2,1)S(1)} collective-permute-done((bf16[32,3584]{1,0:T(8,128)(2,1)S(1)}, bf16[32,3584]{1,0:T(8,128)(2,1)S(1)}, u32[]{:S(2)}, u32[]{:S(2)}) %collective-permute-start.20) | collective-permute-done | bytes 229408 | tf_op jit(solution)/shard_map/ppermute | solution.py:39
  117.1 1.6 collective-permute-done.22
  120.1 8.3 %collective-permute-start.23 = (bf16[128,3584]{1,0:T(8,128)(2,1)S(1)}, bf16[128,3584]{1,0:T(8,128)(2,1)S(1)}, u32[]{:S(2)}, u32[]{:S(2)}) collective-permute-start(bf16[128,3584]{1,0:T(8,128)(2,1)S(1)} %pad_maximum_fusion), channel_id=1, source_target_pairs={{0,8},{8,0},{16,24},{24,16},{32,40},{40,32},{48,56},{56,48},{64,72... | collective-permute-start | bytes 2752520 | tf_op jit(solution)/shard_map/ppermute | solution.py:47
  128.4 2.0 %convolution_convert_fusion.7.proj_ref = bf16[384,256]{1,0:T(8,128)(2,1)} fusion(bf16[384,256]{1,0:T(8,128)(2,1)} %pad_maximum_fusion.4, s32[384]{0:T(512)S(1)} %fusion.34), kind=kOutput, calls=%fused_computation.8 | convolution fusion | flops 75743232 | bytes 394752 | tf_op jit(solution)/shard_map/dot_general | solution.py:270
  130.6 1.8 convolution_convert_fusion.2
  132.4 3.5 %all-to-all-start.2 = ((bf16[8,32,512]{2,1,0:T(8,128)(2,1)}), bf16[8,32,512]{2,1,0:T(8,128)(2,1)S(1)}, u32[]{:S(2)}, u32[]{:S(2)}) async-start(bf16[8,32,512]{2,1,0:T(8,128)(2,1)} %bitcast.9), calls=%async_computation.2 | async-start | bytes 524288 | tf_op jit(solution)/shard_map/all_to_all | solution.py:86
  135.9 2.8 %convolution_convert_fusion.10 = bf16[256,256]{1,0:T(8,128)(2,1)S(1)} fusion(bf16[256,3584]{1,0:T(8,128)(2,1)} %copy-done.3), kind=kOutput, calls=%fused_computation.11 | convolution fusion | flops 469827584 | bytes 1966080 | tf_op jit(solution)/shard_map/dot_general | solution.py:278
  139.3 4.2 %all-to-all-done.2 = bf16[8,32,512]{2,1,0:T(8,128)(2,1)S(1)} async-done(((bf16[8,32,512]{2,1,0:T(8,128)(2,1)}), bf16[8,32,512]{2,1,0:T(8,128)(2,1)S(1)}, u32[]{:S(2)}, u32[]{:S(2)}) %all-to-all-start.2) | async-done | bytes 262176 | tf_op jit(solution)/shard_map/all_to_all | solution.py:86
  144.3 3.5 %all-to-all-start.3 = ((bf16[8,64,512]{2,1,0:T(8,128)(2,1)}), bf16[8,64,512]{2,1,0:T(8,128)(2,1)S(1)}, u32[]{:S(2)}, u32[]{:S(2)}) async-start(bf16[8,64,512]{2,1,0:T(8,128)(2,1)} %fusion.6), calls=%async_computation.3 | async-start | bytes 1048576 | tf_op jit(solution)/shard_map/all_to_all | solution.py:98
  148.3 8.6 %all-to-all-done.3 = bf16[8,64,512]{2,1,0:T(8,128)(2,1)S(1)} async-done(((bf16[8,64,512]{2,1,0:T(8,128)(2,1)}), bf16[8,64,512]{2,1,0:T(8,128)(2,1)S(1)}, u32[]{:S(2)}, u32[]{:S(2)}) %all-to-all-start.3) | async-done | bytes 524320 | tf_op jit(solution)/shard_map/all_to_all | solution.py:98
  157.7 2.1 %collective-permute-start.24 = (bf16[768,256]{1,0:T(8,128)(2,1)S(1)}, bf16[768,256]{1,0:T(8,128)(2,1)S(1)}, u32[]{:S(2)}, u32[]{:S(2)}) collective-permute-start(bf16[768,256]{1,0:T(8,128)(2,1)S(1)} %convolution_convert_fusion), channel_id=1, source_target_pairs={{0,8},{8,0},{16,24},{24,16},{32,40},{40,32},{48,56},{56,48},{64,72... | collective-permute-start | bytes 1179656 | tf_op jit(solution)/shard_map/ppermute | solution.py:47
  159.9 1.3 collective-permute-done.24
  161.7 2.7 %collective-permute-start.26 = (bf16[192,256]{1,0:T(8,128)(2,1)S(1)}, bf16[192,256]{1,0:T(8,128)(2,1)S(1)}, u32[]{:S(2)}, u32[]{:S(2)}) collective-permute-start(bf16[192,256]{1,0:T(8,128)(2,1)S(1)} %get-tuple-element.57), channel_id=1, source_target_pairs={{0,192},{8,200},{16,208},{24,216},{32,224},{40,232},{48,240},{56,2... | collective-permute-start | bytes 294920 | tf_op jit(solution)/shard_map/ppermute | solution.py:39
  164.7 2.3 %collective-permute-done.25 = bf16[192,256]{1,0:T(8,128)(2,1)S(1)} collective-permute-done((bf16[192,256]{1,0:T(8,128)(2,1)S(1)}, bf16[192,256]{1,0:T(8,128)(2,1)S(1)}, u32[]{:S(2)}, u32[]{:S(2)}) %collective-permute-start.25) | collective-permute-done | bytes 98336 | tf_op jit(solution)/shard_map/ppermute | solution.py:39
  167.0 2.1 %collective-permute-done.26 = bf16[192,256]{1,0:T(8,128)(2,1)S(1)} collective-permute-done((bf16[192,256]{1,0:T(8,128)(2,1)S(1)}, bf16[192,256]{1,0:T(8,128)(2,1)S(1)}, u32[]{:S(2)}, u32[]{:S(2)}) %collective-permute-start.26) | collective-permute-done | bytes 98336 | tf_op jit(solution)/shard_map/ppermute | solution.py:39
  170.0 3.6 %collective-permute-start.29 = (bf16[48,256]{1,0:T(8,128)(2,1)S(1)}, bf16[48,256]{1,0:T(8,128)(2,1)S(1)}, u32[]{:S(2)}, u32[]{:S(2)}) collective-permute-start(bf16[48,256]{1,0:T(8,128)(2,1)S(1)} %get-tuple-element.63), channel_id=1, source_target_pairs={{0,48},{8,56},{16,0},{24,8},{32,16},{40,24},{48,32},{56,40},{64,11... | collective-permute-start | bytes 73736 | tf_op jit(solution)/shard_map/ppermute | solution.py:43
  173.6 5.9 %collective-permute-start.30 = (bf16[48,256]{1,0:T(8,128)(2,1)S(1)}, bf16[48,256]{1,0:T(8,128)(2,1)S(1)}, u32[]{:S(2)}, u32[]{:S(2)}) collective-permute-start(bf16[48,256]{1,0:T(8,128)(2,1)S(1)} %get-tuple-element.62), channel_id=1, source_target_pairs={{0,32},{8,40},{16,48},{24,56},{32,0},{40,8},{48,16},{56,24},{64,96... | collective-permute-start | bytes 73736 | tf_op jit(solution)/shard_map/ppermute | solution.py:43
  179.5 5.1 %weights.1 = bf16[384,3584]{1,0:T(8,128)(2,1)} custom-call(bf16[384,256]{1,0:T(8,128)(2,1)} %convolution_convert_fusion.7.proj_ref, bf16[256,3584]{1,0:T(8,128)(2,1)} %all-gather.2.cloned.1.call-done.update_ref, bf16[384,3584]{1,0:T(8,128)(2,1)} %weights_ref.1), custom_call_target="tpu_custom_call" | custom-call | flops 704643072 | bytes 8000000 | tf_op jit(solution)/shard_map/weights/pallas_call | solution.py:197
  (111 shorter events, 18.0 us)
Async XLA Ops:
  8.0 12.8 %collective-permute-start = (bf16[48,256]{1,0:T(8,128)(2,1)S(1)}, bf16[48,256]{1,0:T(8,128)(2,1)S(1)}, u32[]{:S(2)}, u32[]{:S(2)}) collective-permute-start(bf16[48,256]{1,0:T(8,128)(2,1)S(1)} %convert_element_type.178), channel_id=1, source_target_pairs={{0,48},{8,56},{16,0},{24,8},{32,16},{40,24},{48,32},{56,40},{64,11... | collective-permute-start | bytes 73736 | tf_op jit(solution)/shard_map/ppermute | solution.py:43
  14.8 6.6 %collective-permute-start.1 = (bf16[48,256]{1,0:T(8,128)(2,1)S(1)}, bf16[48,256]{1,0:T(8,128)(2,1)S(1)}, u32[]{:S(2)}, u32[]{:S(2)}) collective-permute-start(bf16[48,256]{1,0:T(8,128)(2,1)S(1)} %convert_element_type.178), channel_id=1, source_target_pairs={{0,32},{8,40},{16,48},{24,56},{32,0},{40,8},{48,16},{56,24},{64,96... | collective-permute-start | bytes 73736 | tf_op jit(solution)/shard_map/ppermute | solution.py:43
  15.7 5.7 %collective-permute-start.2 = (bf16[48,256]{1,0:T(8,128)(2,1)S(1)}, bf16[48,256]{1,0:T(8,128)(2,1)S(1)}, u32[]{:S(2)}, u32[]{:S(2)}) collective-permute-start(bf16[48,256]{1,0:T(8,128)(2,1)S(1)} %convert_element_type.178), channel_id=1, source_target_pairs={{0,16},{8,24},{16,32},{24,40},{32,48},{40,56},{48,0},{56,8},{64,80... | collective-permute-start | bytes 73736 | tf_op jit(solution)/shard_map/ppermute | solution.py:43
  18.1 1.4 copy-start.2
  21.4 4.5 %collective-permute-start.3 = (bf16[192,256]{1,0:T(8,128)(2,1)S(1)}, bf16[192,256]{1,0:T(8,128)(2,1)S(1)}, u32[]{:S(2)}, u32[]{:S(2)}) collective-permute-start(bf16[192,256]{1,0:T(8,128)(2,1)S(1)} %pad_maximum_fusion.7), channel_id=1, source_target_pairs={{0,192},{8,200},{16,208},{24,216},{32,224},{40,232},{48,240},{56,2... | collective-permute-start | bytes 294920 | tf_op jit(solution)/shard_map/ppermute | solution.py:39
  24.2 5.1 %collective-permute-start.4 = (bf16[192,256]{1,0:T(8,128)(2,1)S(1)}, bf16[192,256]{1,0:T(8,128)(2,1)S(1)}, u32[]{:S(2)}, u32[]{:S(2)}) collective-permute-start(bf16[192,256]{1,0:T(8,128)(2,1)S(1)} %pad_maximum_fusion.7), channel_id=1, source_target_pairs={{0,128},{8,136},{16,144},{24,152},{32,160},{40,168},{48,176},{56,1... | collective-permute-start | bytes 294920 | tf_op jit(solution)/shard_map/ppermute | solution.py:39
  24.6 5.7 %collective-permute-start.5 = (bf16[192,256]{1,0:T(8,128)(2,1)S(1)}, bf16[192,256]{1,0:T(8,128)(2,1)S(1)}, u32[]{:S(2)}, u32[]{:S(2)}) collective-permute-start(bf16[192,256]{1,0:T(8,128)(2,1)S(1)} %pad_maximum_fusion.7), channel_id=1, source_target_pairs={{0,64},{8,72},{16,80},{24,88},{32,96},{40,104},{48,112},{56,120},{... | collective-permute-start | bytes 294920 | tf_op jit(solution)/shard_map/ppermute | solution.py:39
  30.3 5.0 %collective-permute-start.6 = (bf16[768,256]{1,0:T(8,128)(2,1)S(1)}, bf16[768,256]{1,0:T(8,128)(2,1)S(1)}, u32[]{:S(2)}, u32[]{:S(2)}) collective-permute-start(bf16[768,256]{1,0:T(8,128)(2,1)S(1)} %pad_maximum_fusion.1), channel_id=1, source_target_pairs={{0,8},{8,0},{16,24},{24,16},{32,40},{40,32},{48,56},{56,48},{64,72... | collective-permute-start | bytes 1179656 | tf_op jit(solution)/shard_map/ppermute | solution.py:47
  47.6 9.5 %all-to-all-start.1 = ((bf16[8,32,512]{2,1,0:T(8,128)(2,1)}), bf16[8,32,512]{2,1,0:T(8,128)(2,1)S(1)}, u32[]{:S(2)}, u32[]{:S(2)}) async-start(bf16[8,32,512]{2,1,0:T(8,128)(2,1)} %broadcast_in_dim.19), calls=%async_computation.1 | async-start | bytes 524288 | tf_op jit(solution)/shard_map/all_to_all | solution.py:98
  51.0 128.5 %all-gather.2.cloned.1.call-start = ((), (), s32[]{:S(2)}) async-start(), calls=%async_computation.4 | async-start | bytes 1892352 | tf_op jit(solution)/shard_map/all_gather | solution.py:262
  57.4 2.0 %copy-start = (bf16[512,3584]{1,0:T(8,128)(2,1)S(1)}, bf16[512,3584]{1,0:T(8,128)(2,1)}, u32[]{:S(2)}) copy-start(bf16[512,3584]{1,0:T(8,128)(2,1)} %cot_ref.1) | copy-start | bytes 11010052
  60.6 4.8 %collective-permute-start.7 = (bf16[128,3584]{1,0:T(8,128)(2,1)S(1)}, bf16[128,3584]{1,0:T(8,128)(2,1)S(1)}, u32[]{:S(2)}, u32[]{:S(2)}) collective-permute-start(bf16[128,3584]{1,0:T(8,128)(2,1)S(1)} %get-tuple-element.24), channel_id=1, source_target_pairs={{0,8},{8,0},{16,24},{24,16},{32,40},{40,32},{48,56},{56,48},{64,72... | collective-permute-start | bytes 2752520 | tf_op jit(solution)/shard_map/ppermute | solution.py:47
  65.7 13.0 %collective-permute-start.8 = (bf16[32,3584]{1,0:T(8,128)(2,1)S(1)}, bf16[32,3584]{1,0:T(8,128)(2,1)S(1)}, u32[]{:S(2)}, u32[]{:S(2)}) collective-permute-start(bf16[32,3584]{1,0:T(8,128)(2,1)S(1)} %get-tuple-element.52), channel_id=1, source_target_pairs={{0,64},{8,72},{16,80},{24,88},{32,96},{40,104},{48,112},{56,120},{... | collective-permute-start | bytes 688136 | tf_op jit(solution)/shard_map/ppermute | solution.py:39
  65.8 13.5 %collective-permute-start.10 = (bf16[32,3584]{1,0:T(8,128)(2,1)S(1)}, bf16[32,3584]{1,0:T(8,128)(2,1)S(1)}, u32[]{:S(2)}, u32[]{:S(2)}) collective-permute-start(bf16[32,3584]{1,0:T(8,128)(2,1)S(1)} %get-tuple-element.53), channel_id=1, source_target_pairs={{0,128},{8,136},{16,144},{24,152},{32,160},{40,168},{48,176},{56,1... | collective-permute-start | bytes 688136 | tf_op jit(solution)/shard_map/ppermute | solution.py:39
  67.3 12.0 %collective-permute-start.9 = (bf16[32,3584]{1,0:T(8,128)(2,1)S(1)}, bf16[32,3584]{1,0:T(8,128)(2,1)S(1)}, u32[]{:S(2)}, u32[]{:S(2)}) collective-permute-start(bf16[32,3584]{1,0:T(8,128)(2,1)S(1)} %get-tuple-element.54), channel_id=1, source_target_pairs={{0,192},{8,200},{16,208},{24,216},{32,224},{40,232},{48,240},{56,2... | collective-permute-start | bytes 688136 | tf_op jit(solution)/shard_map/ppermute | solution.py:39
  78.8 4.5 %collective-permute-start.11 = (bf16[320,256]{1,0:T(8,128)(2,1)S(1)}, bf16[320,256]{1,0:T(8,128)(2,1)S(1)}, u32[]{:S(2)}, u32[]{:S(2)}) collective-permute-start(bf16[320,256]{1,0:T(8,128)(2,1)S(1)} %pad_maximum_fusion.6), channel_id=1, source_target_pairs={{0,1},{1,0},{2,3},{3,2},{4,5},{5,4},{6,7},{7,6},{8,9},{9,8},{10,11... | collective-permute-start | bytes 491528 | tf_op jit(solution)/shard_map/ppermute | solution.py:51
  79.3 15.8 %copy-start.6 = (f32[8,3584]{1,0:T(8,128)S(1)}, f32[8,3584]{1,0:T(8,128)}, u32[]{:S(2)}) copy-start(f32[8,3584]{1,0:T(8,128)} %param.10) | copy-start | bytes 344068
  79.3 15.8 %copy-start.7 = (f32[8,3584]{1,0:T(8,128)S(1)}, f32[8,3584]{1,0:T(8,128)}, u32[]{:S(2)}) copy-start(f32[8,3584]{1,0:T(8,128)} %param.11) | copy-start | bytes 344068
  83.4 7.6 %collective-permute-start.12 = (bf16[8,3584]{1,0:T(8,128)(2,1)S(1)}, bf16[8,3584]{1,0:T(8,128)(2,1)S(1)}, u32[]{:S(2)}, u32[]{:S(2)}) collective-permute-start(bf16[8,3584]{1,0:T(8,128)(2,1)S(1)} %get-tuple-element.58), channel_id=1, source_target_pairs={{0,16},{8,24},{16,32},{24,40},{32,48},{40,56},{48,0},{56,8},{64,80... | collective-permute-start | bytes 172040 | tf_op jit(solution)/shard_map/ppermute | solution.py:43
  84.6 6.3 %collective-permute-start.13 = (bf16[8,3584]{1,0:T(8,128)(2,1)S(1)}, bf16[8,3584]{1,0:T(8,128)(2,1)S(1)}, u32[]{:S(2)}, u32[]{:S(2)}) collective-permute-start(bf16[8,3584]{1,0:T(8,128)(2,1)S(1)} %get-tuple-element.60), channel_id=1, source_target_pairs={{0,48},{8,56},{16,0},{24,8},{32,16},{40,24},{48,32},{56,40},{64,11... | collective-permute-start | bytes 172040 | tf_op jit(solution)/shard_map/ppermute | solution.py:43
  87.0 8.1 %collective-permute-start.14 = (bf16[8,3584]{1,0:T(8,128)(2,1)S(1)}, bf16[8,3584]{1,0:T(8,128)(2,1)S(1)}, u32[]{:S(2)}, u32[]{:S(2)}) collective-permute-start(bf16[8,3584]{1,0:T(8,128)(2,1)S(1)} %get-tuple-element.59), channel_id=1, source_target_pairs={{0,32},{8,40},{16,48},{24,56},{32,0},{40,8},{48,16},{56,24},{64,96... | collective-permute-start | bytes 172040 | tf_op jit(solution)/shard_map/ppermute | solution.py:43
  95.9 5.6 %collective-permute-start.15 = (bf16[8,3584]{1,0:T(8,128)(2,1)S(1)}, bf16[8,3584]{1,0:T(8,128)(2,1)S(1)}, u32[]{:S(2)}, u32[]{:S(2)}) collective-permute-start(bf16[8,3584]{1,0:T(8,128)(2,1)S(1)} %get-tuple-element.43), channel_id=1, source_target_pairs={{0,48},{8,56},{16,0},{24,8},{32,16},{40,24},{48,32},{56,40},{64,11... | collective-permute-start | bytes 172040 | tf_op jit(solution)/shard_map/ppermute | solution.py:43
  96.1 7.0 %collective-permute-start.16 = (bf16[8,3584]{1,0:T(8,128)(2,1)S(1)}, bf16[8,3584]{1,0:T(8,128)(2,1)S(1)}, u32[]{:S(2)}, u32[]{:S(2)}) collective-permute-start(bf16[8,3584]{1,0:T(8,128)(2,1)S(1)} %get-tuple-element.43), channel_id=1, source_target_pairs={{0,32},{8,40},{16,48},{24,56},{32,0},{40,8},{48,16},{56,24},{64,96... | collective-permute-start | bytes 172040 | tf_op jit(solution)/shard_map/ppermute | solution.py:43
  99.0 5.8 %collective-permute-start.17 = (bf16[8,3584]{1,0:T(8,128)(2,1)S(1)}, bf16[8,3584]{1,0:T(8,128)(2,1)S(1)}, u32[]{:S(2)}, u32[]{:S(2)}) collective-permute-start(bf16[8,3584]{1,0:T(8,128)(2,1)S(1)} %get-tuple-element.43), channel_id=1, source_target_pairs={{0,16},{8,24},{16,32},{24,40},{32,48},{40,56},{48,0},{56,8},{64,80... | collective-permute-start | bytes 172040 | tf_op jit(solution)/shard_map/ppermute | solution.py:43
  101.4 4.5 %collective-permute-start.18 = (bf16[368,256]{1,0:T(8,128)(2,1)S(1)}, bf16[368,256]{1,0:T(8,128)(2,1)S(1)}, u32[]{:S(2)}, u32[]{:S(2)}) collective-permute-start(bf16[368,256]{1,0:T(8,128)(2,1)S(1)} %pad_maximum_fusion.5), channel_id=1, source_target_pairs={{0,2},{1,3},{2,0},{3,1},{4,6},{5,7},{6,4},{7,5},{8,10},{9,11},{10,... | collective-permute-start | bytes 565256 | tf_op jit(solution)/shard_map/ppermute | solution.py:51
  106.0 6.2 %collective-permute-start.21 = (bf16[32,3584]{1,0:T(8,128)(2,1)S(1)}, bf16[32,3584]{1,0:T(8,128)(2,1)S(1)}, u32[]{:S(2)}, u32[]{:S(2)}) collective-permute-start(bf16[32,3584]{1,0:T(8,128)(2,1)S(1)} %pad_maximum_fusion.3), channel_id=1, source_target_pairs={{0,64},{8,72},{16,80},{24,88},{32,96},{40,104},{48,112},{56,120},{... | collective-permute-start | bytes 688136 | tf_op jit(solution)/shard_map/ppermute | solution.py:39
  106.1 8.1 %collective-permute-start.19 = (bf16[32,3584]{1,0:T(8,128)(2,1)S(1)}, bf16[32,3584]{1,0:T(8,128)(2,1)S(1)}, u32[]{:S(2)}, u32[]{:S(2)}) collective-permute-start(bf16[32,3584]{1,0:T(8,128)(2,1)S(1)} %pad_maximum_fusion.3), channel_id=1, source_target_pairs={{0,192},{8,200},{16,208},{24,216},{32,224},{40,232},{48,240},{56,2... | collective-permute-start | bytes 688136 | tf_op jit(solution)/shard_map/ppermute | solution.py:39
  108.8 8.2 %collective-permute-start.20 = (bf16[32,3584]{1,0:T(8,128)(2,1)S(1)}, bf16[32,3584]{1,0:T(8,128)(2,1)S(1)}, u32[]{:S(2)}, u32[]{:S(2)}) collective-permute-start(bf16[32,3584]{1,0:T(8,128)(2,1)S(1)} %pad_maximum_fusion.3), channel_id=1, source_target_pairs={{0,128},{8,136},{16,144},{24,152},{32,160},{40,168},{48,176},{56,1... | collective-permute-start | bytes 688136 | tf_op jit(solution)/shard_map/ppermute | solution.py:39
  112.2 6.5 %collective-permute-start.22 = (bf16[464,256]{1,0:T(8,128)(2,1)S(1)}, bf16[464,256]{1,0:T(8,128)(2,1)S(1)}, u32[]{:S(2)}, u32[]{:S(2)}) collective-permute-start(bf16[464,256]{1,0:T(8,128)(2,1)S(1)} %pad_maximum_fusion.2), channel_id=1, source_target_pairs={{0,6},{1,7},{2,4},{3,5},{4,2},{5,3},{6,0},{7,1},{8,14},{9,15},{10,... | collective-permute-start | bytes 712712 | tf_op jit(solution)/shard_map/ppermute | solution.py:51
  120.1 10.4 %collective-permute-start.23 = (bf16[128,3584]{1,0:T(8,128)(2,1)S(1)}, bf16[128,3584]{1,0:T(8,128)(2,1)S(1)}, u32[]{:S(2)}, u32[]{:S(2)}) collective-permute-start(bf16[128,3584]{1,0:T(8,128)(2,1)S(1)} %pad_maximum_fusion), channel_id=1, source_target_pairs={{0,8},{8,0},{16,24},{24,16},{32,40},{40,32},{48,56},{56,48},{64,72... | collective-permute-start | bytes 2752520 | tf_op jit(solution)/shard_map/ppermute | solution.py:47
  128.4 2.2 %copy-start.1 = (bf16[512,3584]{1,0:T(8,128)(2,1)S(1)}, bf16[512,3584]{1,0:T(8,128)(2,1)}, u32[]{:S(2)}) copy-start(bf16[512,3584]{1,0:T(8,128)(2,1)} %cot_ref.1) | copy-start | bytes 11010052
  130.6 1.9 copy-start.3
  132.4 11.0 %all-to-all-start.2 = ((bf16[8,32,512]{2,1,0:T(8,128)(2,1)}), bf16[8,32,512]{2,1,0:T(8,128)(2,1)S(1)}, u32[]{:S(2)}, u32[]{:S(2)}) async-start(bf16[8,32,512]{2,1,0:T(8,128)(2,1)} %bitcast.9), calls=%async_computation.2 | async-start | bytes 524288 | tf_op jit(solution)/shard_map/all_to_all | solution.py:86
  135.9 2.8 %copy-start.5 = (bf16[384,256]{1,0:T(8,128)(2,1)S(1)}, bf16[384,256]{1,0:T(8,128)(2,1)}, u32[]{:S(2)}) copy-start(bf16[384,256]{1,0:T(8,128)(2,1)} %convolution_convert_fusion.7.proj_ref) | copy-start | bytes 589828
  138.7 9.2 %copy-start.4 = (f32[256,256]{1,0:T(8,128)S(1)}, f32[256,256]{1,0:T(8,128)}, u32[]{:S(2)}) copy-start(f32[256,256]{1,0:T(8,128)} %select_add_fusion) | copy-start | bytes 786436
  144.3 12.6 %all-to-all-start.3 = ((bf16[8,64,512]{2,1,0:T(8,128)(2,1)}), bf16[8,64,512]{2,1,0:T(8,128)(2,1)S(1)}, u32[]{:S(2)}, u32[]{:S(2)}) async-start(bf16[8,64,512]{2,1,0:T(8,128)(2,1)} %fusion.6), calls=%async_computation.3 | async-start | bytes 1048576 | tf_op jit(solution)/shard_map/all_to_all | solution.py:98
  157.7 3.5 %collective-permute-start.24 = (bf16[768,256]{1,0:T(8,128)(2,1)S(1)}, bf16[768,256]{1,0:T(8,128)(2,1)S(1)}, u32[]{:S(2)}, u32[]{:S(2)}) collective-permute-start(bf16[768,256]{1,0:T(8,128)(2,1)S(1)} %convolution_convert_fusion), channel_id=1, source_target_pairs={{0,8},{8,0},{16,24},{24,16},{32,40},{40,32},{48,56},{56,48},{64,72... | collective-permute-start | bytes 1179656 | tf_op jit(solution)/shard_map/ppermute | solution.py:47
  161.6 5.4 %collective-permute-start.25 = (bf16[192,256]{1,0:T(8,128)(2,1)S(1)}, bf16[192,256]{1,0:T(8,128)(2,1)S(1)}, u32[]{:S(2)}, u32[]{:S(2)}) collective-permute-start(bf16[192,256]{1,0:T(8,128)(2,1)S(1)} %get-tuple-element.55), channel_id=1, source_target_pairs={{0,64},{8,72},{16,80},{24,88},{32,96},{40,104},{48,112},{56,120},{... | collective-permute-start | bytes 294920 | tf_op jit(solution)/shard_map/ppermute | solution.py:39
  161.7 7.4 %collective-permute-start.26 = (bf16[192,256]{1,0:T(8,128)(2,1)S(1)}, bf16[192,256]{1,0:T(8,128)(2,1)S(1)}, u32[]{:S(2)}, u32[]{:S(2)}) collective-permute-start(bf16[192,256]{1,0:T(8,128)(2,1)S(1)} %get-tuple-element.57), channel_id=1, source_target_pairs={{0,192},{8,200},{16,208},{24,216},{32,224},{40,232},{48,240},{56,2... | collective-permute-start | bytes 294920 | tf_op jit(solution)/shard_map/ppermute | solution.py:39
  164.4 5.5 %collective-permute-start.27 = (bf16[192,256]{1,0:T(8,128)(2,1)S(1)}, bf16[192,256]{1,0:T(8,128)(2,1)S(1)}, u32[]{:S(2)}, u32[]{:S(2)}) collective-permute-start(bf16[192,256]{1,0:T(8,128)(2,1)S(1)} %get-tuple-element.56), channel_id=1, source_target_pairs={{0,128},{8,136},{16,144},{24,152},{32,160},{40,168},{48,176},{56,1... | collective-permute-start | bytes 294920 | tf_op jit(solution)/shard_map/ppermute | solution.py:39
  170.0 14.6 %collective-permute-start.28 = (bf16[48,256]{1,0:T(8,128)(2,1)S(1)}, bf16[48,256]{1,0:T(8,128)(2,1)S(1)}, u32[]{:S(2)}, u32[]{:S(2)}) collective-permute-start(bf16[48,256]{1,0:T(8,128)(2,1)S(1)} %get-tuple-element.61), channel_id=1, source_target_pairs={{0,16},{8,24},{16,32},{24,40},{32,48},{40,56},{48,0},{56,8},{64,80... | collective-permute-start | bytes 73736 | tf_op jit(solution)/shard_map/ppermute | solution.py:43
  170.0 14.5 %collective-permute-start.29 = (bf16[48,256]{1,0:T(8,128)(2,1)S(1)}, bf16[48,256]{1,0:T(8,128)(2,1)S(1)}, u32[]{:S(2)}, u32[]{:S(2)}) collective-permute-start(bf16[48,256]{1,0:T(8,128)(2,1)S(1)} %get-tuple-element.63), channel_id=1, source_target_pairs={{0,48},{8,56},{16,0},{24,8},{32,16},{40,24},{48,32},{56,40},{64,11... | collective-permute-start | bytes 73736 | tf_op jit(solution)/shard_map/ppermute | solution.py:43
  173.6 11.0 %collective-permute-start.30 = (bf16[48,256]{1,0:T(8,128)(2,1)S(1)}, bf16[48,256]{1,0:T(8,128)(2,1)S(1)}, u32[]{:S(2)}, u32[]{:S(2)}) collective-permute-start(bf16[48,256]{1,0:T(8,128)(2,1)S(1)} %get-tuple-element.62), channel_id=1, source_target_pairs={{0,32},{8,40},{16,48},{24,56},{32,0},{40,8},{48,16},{56,24},{64,96... | collective-permute-start | bytes 73736 | tf_op jit(solution)/shard_map/ppermute | solution.py:43
Sparse Core Ops, SparseCore 0:
  128.5 49.7 all-gather.1

commit v2 on v1

--- a/solution.py
+++ b/solution.py
@@ -52,7 +52,7 @@
 
 
 def ring_blocks(block, send):
-    got = {k: send(block, k) for k in (1, 3, 2)}
+    got = {k: send(block, k) for k in (2, 1, 3)}
     return jnp.concatenate([block, got[3], got[2], got[1]], axis=0), got[1]
 
 
@@ -69,13 +69,13 @@
     return high, (value - high.astype(f32)).astype(bf16)
 
 
-def side_step(gram, rows, mask, trigger):
+def side_step(gram, rows, mask):
     n = gram.shape[0]
     eye = jnp.eye(n, dtype=f32)
     high, low = split_high(gram)
     rest = jnp.sum(low.astype(f32) * eye, axis=0).astype(bf16)
     payload = jnp.concatenate([high, jnp.broadcast_to(rest, (16, n)), rows], axis=0)
-    got = send_xor(after(payload, trigger), mask)
+    got = send_xor(payload, mask)
     gram = gram + got[:n].astype(f32) + eye * got[n : n + 1].astype(f32)
     return gram, jnp.concatenate([rows, got[n + 16 :]], axis=0)
 
@@ -102,13 +102,13 @@
 
 def reduce_blocks(rows, send, beside=None):
     n = rows.shape[0] // 4
-    got = [send(rows[k * n : (k + 1) * n].astype(bf16), k) for k in (1, 3, 2)]
+    got = [send(rows[k * n : (k + 1) * n].astype(bf16), k) for k in (2, 1, 3)]
     total = rows[:n].astype(f32)
     if beside is not None:
         total = after(total, beside)
     for block in got:
         total = total + block.astype(f32)
-    return total, got[0]
+    return total, got[1]
 
 
 def reduce_ring(rows, send):
@@ -250,19 +250,19 @@
 
     grad_keep, grad_send = gradient_parts(latent_p, out_grads)
     total = grad_keep + send_core(grad_send).astype(f32)
-    total, first_got = reduce_blocks(total, send_y)
-    side = side_step(gram_part, proj_half, 1, first_got)
+    side = after((gram_part, proj_half), total)
+    total = reduce_ring(total, send_y)
+    for mask in (1, 2):
+        side = side_step(*side, mask)
     total, *side = lax.optimization_barrier((total, *side))
     gradient, first_got = reduce_blocks(total, send_z)
-    side = side_step(*side, 2, first_got)
     grad_half = gradient.astype(bf16)
     new_first, new_second, update = adam_rows(gradient, moment_first, moment_second)
-    grad_own, first_got = ring_blocks(grad_half, send_z)
-    grad_own, *side = lax.optimization_barrier((grad_own, *side))
+    grad_own = gather_ring(grad_half, send_z)
+    side = side_step(*side, 6)
+    grad_own, gram_q, proj_rows = lax.optimization_barrier((grad_own, *side))
     update_all = lax.all_gather(update, "dp", axis=0, tiled=True)
-    grad_own, first_got = ring_blocks(grad_own, send_y)
-    side = side_step(*side, 6, first_got)
-    grad_own, gram_q, proj_rows = lax.optimization_barrier((grad_own, *side))
+    grad_own = gather_ring(grad_own, send_y)
     grad_p = jnp.concatenate([grad_own, send_core(grad_own)], axis=0)
     place = jnp.arange(8 * projector.shape[0], dtype=jnp.int32)
     block = place // block_width

time: 194 us -> 187 us (0.964)
  starting transfers between devices: 73.2 us -> 62.9 us
  waiting for transfers between devices: 65.7 us -> 69.6 us
    ppermute x4, starting transfers between devices: 16.7 us -> 9.84 us  [send_core(): return lax.ppermute(block, 'dp', dp_pairs(0, 0, 1))]
    all_to_all x2, waiting for transfers between devices: 14.7 us -> 18.8 us  [spread(): got = lax.all_to_all(blocks, 'tensor', 0, 0)]
    ppermute x12, starting transfers between devices: 32.6 us -> 29.4 us  [send_z(): return lax.ppermute(block, 'dp', dp_pairs(0, k, 0))]
  transfers between devices with their start and end apart: 35 -> 35, of which waited for: 23 -> 25; matrix products, arithmetic and copies ran while one was open for 6% -> 6% of each run, Pallas kernels for 3% -> 3%
where the time goes in v2:
time: 187 us; the launch traced here: 186 us
  waiting for transfers between devices  69.6 us (37%)
  starting transfers between devices  62.9 us (34%)
  between operations  14.5 us (8%)
  blocking collectives  11 us (6%)
  matrix products  9.77 us (5%)
  Pallas kernels  8.27 us (4%)
  other arithmetic  5.35 us (3%)
  local copies, waits for them, and re-layouts  4.91 us (3%)
    ppermute x12, starting transfers between devices, send_z(): return lax.ppermute(block, 'dp', dp_pairs(0, k, 0))  29.4 us
    ppermute x12, waiting for transfers between devices, send_y(): return lax.ppermute(block, 'dp', dp_pairs(k, 0, 0))  29.3 us
    all_to_all x2, waiting for transfers between devices, spread(): got = lax.all_to_all(blocks, 'tensor', 0, 0)  18.8 us
    ppermute x12, starting transfers between devices, send_y(): return lax.ppermute(block, 'dp', dp_pairs(k, 0, 0))  11.2 us
    all_to_all x1, blocking collectives, split_sum(): lax.all_to_all(part.astype(bf16).reshape(n, rows // n, cols), 'tensor', 0...  11 us
    ppermute x4, starting transfers between devices, send_core(): return lax.ppermute(block, 'dp', dp_pairs(0, 0, 1))  9.84 us
    ppermute x12, waiting for transfers between devices, send_z(): return lax.ppermute(block, 'dp', dp_pairs(0, k, 0))  7.55 us
    all_to_all x2, starting transfers between devices, spread(): got = lax.all_to_all(blocks, 'tensor', 0, 0)  6.91 us
  transfers between devices with their start and end apart: 35, of which 25 were waited for; matrix products, arithmetic and copies ran while one was open for 6% of the time, Pallas kernels for 3%

profile of v2, /device:TPU:1, one launch (start us, length us, event | category | flops | bytes accessed | tf_op | source)
XLA Modules:
  0.0 186.3 jit_solution(12841539891452910101)
XLA Ops:
  8.0 6.8 %collective-permute-start = (bf16[48,256]{1,0:T(8,128)(2,1)S(1)}, bf16[48,256]{1,0:T(8,128)(2,1)S(1)}, u32[]{:S(2)}, u32[]{:S(2)}) collective-permute-start(bf16[48,256]{1,0:T(8,128)(2,1)S(1)} %convert_element_type.178), channel_id=1, source_target_pairs={{0,48},{8,56},{16,0},{24,8},{32,16},{40,24},{48,32},{56,40},{64,11... | collective-permute-start | bytes 73736 | tf_op jit(solution)/shard_map/ppermute | solution.py:43
  15.7 2.4 %collective-permute-start.2 = (bf16[48,256]{1,0:T(8,128)(2,1)S(1)}, bf16[48,256]{1,0:T(8,128)(2,1)S(1)}, u32[]{:S(2)}, u32[]{:S(2)}) collective-permute-start(bf16[48,256]{1,0:T(8,128)(2,1)S(1)} %convert_element_type.178), channel_id=1, source_target_pairs={{0,16},{8,24},{16,32},{24,40},{32,48},{40,56},{48,0},{56,8},{64,80... | collective-permute-start | bytes 73736 | tf_op jit(solution)/shard_map/ppermute | solution.py:43
  18.2 1.4 copy-done.2
  21.4 2.8 %collective-permute-start.3 = (bf16[192,256]{1,0:T(8,128)(2,1)S(1)}, bf16[192,256]{1,0:T(8,128)(2,1)S(1)}, u32[]{:S(2)}, u32[]{:S(2)}) collective-permute-start(bf16[192,256]{1,0:T(8,128)(2,1)S(1)} %pad_maximum_fusion.7), channel_id=1, source_target_pairs={{0,192},{8,200},{16,208},{24,216},{32,224},{40,232},{48,240},{56,2... | collective-permute-start | bytes 294920 | tf_op jit(solution)/shard_map/ppermute | solution.py:39
  25.9 3.4 %collective-permute-done.4 = bf16[192,256]{1,0:T(8,128)(2,1)S(1)} collective-permute-done((bf16[192,256]{1,0:T(8,128)(2,1)S(1)}, bf16[192,256]{1,0:T(8,128)(2,1)S(1)}, u32[]{:S(2)}, u32[]{:S(2)}) %collective-permute-start.4) | collective-permute-done | bytes 98336 | tf_op jit(solution)/shard_map/ppermute | solution.py:39
  30.3 3.6 %collective-permute-start.6 = (bf16[768,256]{1,0:T(8,128)(2,1)S(1)}, bf16[768,256]{1,0:T(8,128)(2,1)S(1)}, u32[]{:S(2)}, u32[]{:S(2)}) collective-permute-start(bf16[768,256]{1,0:T(8,128)(2,1)S(1)} %pad_maximum_fusion.1), channel_id=1, source_target_pairs={{0,8},{8,0},{16,24},{24,16},{32,40},{40,32},{48,56},{56,48},{64,72... | collective-permute-start | bytes 1179656 | tf_op jit(solution)/shard_map/ppermute | solution.py:47
  34.0 1.3 collective-permute-done.6
  36.2 11.0 %all_to_all.20 = bf16[8,32,512]{2,1,0:T(8,128)(2,1)S(1)} all-to-all(bf16[8,32,512]{2,1,0:T(8,128)(2,1)S(1)} %bitcast.27), channel_id=1, replica_groups=mesh['dp'=32,'tensor'=8] {'tensor'}, dimensions={0} | all-to-all | bytes 524288 | tf_op jit(solution)/shard_map/all_to_all | solution.py:86
  47.9 3.4 %all-to-all-start.1 = ((bf16[8,32,512]{2,1,0:T(8,128)(2,1)}), bf16[8,32,512]{2,1,0:T(8,128)(2,1)S(1)}, u32[]{:S(2)}, u32[]{:S(2)}) async-start(bf16[8,32,512]{2,1,0:T(8,128)(2,1)} %broadcast_in_dim.19), calls=%async_computation.1 | async-start | bytes 524288 | tf_op jit(solution)/shard_map/all_to_all | solution.py:98
  51.4 6.0 %all-to-all-done.1 = bf16[8,32,512]{2,1,0:T(8,128)(2,1)S(1)} async-done(((bf16[8,32,512]{2,1,0:T(8,128)(2,1)}), bf16[8,32,512]{2,1,0:T(8,128)(2,1)S(1)}, u32[]{:S(2)}, u32[]{:S(2)}) %all-to-all-start.1) | async-done | bytes 262176 | tf_op jit(solution)/shard_map/all_to_all | solution.py:98
  57.7 2.0 %copy-done = bf16[512,3584]{1,0:T(8,128)(2,1)S(1)} copy-done((bf16[512,3584]{1,0:T(8,128)(2,1)S(1)}, bf16[512,3584]{1,0:T(8,128)(2,1)}, u32[]{:S(2)}) %copy-start) | copy-done | bytes 3670040
  59.8 2.0 %gradient.1 = (f32[128,3584]{1,0:T(8,128)S(1)}, bf16[128,3584]{1,0:T(8,128)(2,1)}) custom-call(bf16[256,512]{1,0:T(8,128)(2,1)S(1)} %convolution_convert_fusion.3.latent_ref, bf16[512,3584]{1,0:T(8,128)(2,1)S(1)} %copy-done), custom_call_target="tpu_custom_call" | custom-call | flops 939524096 | bytes 6500000 | tf_op jit(solution)/shard_map/gradient/pallas_call | solution.py:172
  61.8 2.6 %collective-permute-start.7 = (bf16[128,3584]{1,0:T(8,128)(2,1)}, bf16[128,3584]{1,0:T(8,128)(2,1)}, u32[]{:S(2)}, u32[]{:S(2)}) collective-permute-start(bf16[128,3584]{1,0:T(8,128)(2,1)} %get-tuple-element.20), channel_id=1, source_target_pairs={{0,8},{8,0},{16,24},{24,16},{32,40},{40,32},{48,56},{56,48},{64,72... | collective-permute-start | bytes 2752520 | tf_op jit(solution)/shard_map/ppermute | solution.py:47
  64.5 1.8 fusion.69
  66.9 1.4 fusion.63
  70.7 3.2 %collective-permute-done.11 = bf16[320,256]{1,0:T(8,128)(2,1)S(1)} collective-permute-done((bf16[320,256]{1,0:T(8,128)(2,1)S(1)}, bf16[320,256]{1,0:T(8,128)(2,1)S(1)}, u32[]{:S(2)}, u32[]{:S(2)}) %collective-permute-start.11) | collective-permute-done | bytes 163872 | tf_op jit(solution)/shard_map/ppermute | solution.py:51
  74.1 1.5 collective-permute-done.10
  75.7 1.5 collective-permute-done.8
  77.2 6.2 %collective-permute-done.9 = bf16[32,3584]{1,0:T(8,128)(2,1)S(1)} collective-permute-done((bf16[32,3584]{1,0:T(8,128)(2,1)S(1)}, bf16[32,3584]{1,0:T(8,128)(2,1)S(1)}, u32[]{:S(2)}, u32[]{:S(2)}) %collective-permute-start.9) | collective-permute-done | bytes 229408 | tf_op jit(solution)/shard_map/ppermute | solution.py:39
  83.7 4.1 %collective-permute-start.13 = (bf16[8,3584]{1,0:T(8,128)(2,1)S(1)}, bf16[8,3584]{1,0:T(8,128)(2,1)S(1)}, u32[]{:S(2)}, u32[]{:S(2)}) collective-permute-start(bf16[8,3584]{1,0:T(8,128)(2,1)S(1)} %get-tuple-element.50), channel_id=1, source_target_pairs={{0,32},{8,40},{16,48},{24,56},{32,0},{40,8},{48,16},{56,24},{64,96... | collective-permute-start | bytes 172040 | tf_op jit(solution)/shard_map/ppermute | solution.py:43
  87.8 3.6 %collective-permute-start.15 = (bf16[8,3584]{1,0:T(8,128)(2,1)S(1)}, bf16[8,3584]{1,0:T(8,128)(2,1)S(1)}, u32[]{:S(2)}, u32[]{:S(2)}) collective-permute-start(bf16[8,3584]{1,0:T(8,128)(2,1)S(1)} %get-tuple-element.51), channel_id=1, source_target_pairs={{0,48},{8,56},{16,0},{24,8},{32,16},{40,24},{48,32},{56,40},{64,11... | collective-permute-start | bytes 172040 | tf_op jit(solution)/shard_map/ppermute | solution.py:43
  91.4 1.9 %collective-permute-done.14 = bf16[8,3584]{1,0:T(8,128)(2,1)S(1)} collective-permute-done((bf16[8,3584]{1,0:T(8,128)(2,1)S(1)}, bf16[8,3584]{1,0:T(8,128)(2,1)S(1)}, u32[]{:S(2)}, u32[]{:S(2)}) %collective-permute-start.14) | collective-permute-done | bytes 57376 | tf_op jit(solution)/shard_map/ppermute | solution.py:43
  95.4 1.9 %collective-permute-start.16 = (bf16[8,3584]{1,0:T(8,128)(2,1)S(1)}, bf16[8,3584]{1,0:T(8,128)(2,1)S(1)}, u32[]{:S(2)}, u32[]{:S(2)}) collective-permute-start(bf16[8,3584]{1,0:T(8,128)(2,1)S(1)} %get-tuple-element.35), channel_id=1, source_target_pairs={{0,48},{8,56},{16,0},{24,8},{32,16},{40,24},{48,32},{56,40},{64,11... | collective-permute-start | bytes 172040 | tf_op jit(solution)/shard_map/ppermute | solution.py:43
  97.3 1.8 collective-permute-start.17
  99.1 1.9 %collective-permute-start.18 = (bf16[8,3584]{1,0:T(8,128)(2,1)S(1)}, bf16[8,3584]{1,0:T(8,128)(2,1)S(1)}, u32[]{:S(2)}, u32[]{:S(2)}) collective-permute-start(bf16[8,3584]{1,0:T(8,128)(2,1)S(1)} %get-tuple-element.35), channel_id=1, source_target_pairs={{0,16},{8,24},{16,32},{24,40},{32,48},{40,56},{48,0},{56,8},{64,80... | collective-permute-start | bytes 172040 | tf_op jit(solution)/shard_map/ppermute | solution.py:43
  102.4 2.0 %collective-permute-done.17 = bf16[8,3584]{1,0:T(8,128)(2,1)S(1)} collective-permute-done((bf16[8,3584]{1,0:T(8,128)(2,1)S(1)}, bf16[8,3584]{1,0:T(8,128)(2,1)S(1)}, u32[]{:S(2)}, u32[]{:S(2)}) %collective-permute-start.17) | collective-permute-done | bytes 57376 | tf_op jit(solution)/shard_map/ppermute | solution.py:43
  104.4 1.6 collective-permute-done.18
  106.1 1.8 collective-permute-done.19
  109.9 3.1 %collective-permute-done.20 = bf16[32,3584]{1,0:T(8,128)(2,1)S(1)} collective-permute-done((bf16[32,3584]{1,0:T(8,128)(2,1)S(1)}, bf16[32,3584]{1,0:T(8,128)(2,1)S(1)}, u32[]{:S(2)}, u32[]{:S(2)}) %collective-permute-start.20) | collective-permute-done | bytes 229408 | tf_op jit(solution)/shard_map/ppermute | solution.py:39
  113.0 1.7 collective-permute-done.21
  114.7 6.7 %collective-permute-done.22 = bf16[32,3584]{1,0:T(8,128)(2,1)S(1)} collective-permute-done((bf16[32,3584]{1,0:T(8,128)(2,1)S(1)}, bf16[32,3584]{1,0:T(8,128)(2,1)S(1)}, u32[]{:S(2)}, u32[]{:S(2)}) %collective-permute-start.22) | collective-permute-done | bytes 229408 | tf_op jit(solution)/shard_map/ppermute | solution.py:39
  121.4 1.9 %collective-permute-start.23 = (bf16[128,3584]{1,0:T(8,128)(2,1)S(1)}, bf16[128,3584]{1,0:T(8,128)(2,1)S(1)}, u32[]{:S(2)}, u32[]{:S(2)}) collective-permute-start(bf16[128,3584]{1,0:T(8,128)(2,1)S(1)} %pad_maximum_fusion), channel_id=1, source_target_pairs={{0,8},{8,0},{16,24},{24,16},{32,40},{40,32},{48,56},{56,48},{64,72... | collective-permute-start | bytes 2752520 | tf_op jit(solution)/shard_map/ppermute | solution.py:47
  123.4 2.0 %collective-permute-done.23 = bf16[128,3584]{1,0:T(8,128)(2,1)S(1)} collective-permute-done((bf16[128,3584]{1,0:T(8,128)(2,1)S(1)}, bf16[128,3584]{1,0:T(8,128)(2,1)S(1)}, u32[]{:S(2)}, u32[]{:S(2)}) %collective-permute-start.23) | collective-permute-done | bytes 917536 | tf_op jit(solution)/shard_map/ppermute | solution.py:47
  125.5 1.9 convolution_convert_fusion.2
  127.4 3.4 %all-to-all-start.2 = ((bf16[8,32,512]{2,1,0:T(8,128)(2,1)}), bf16[8,32,512]{2,1,0:T(8,128)(2,1)S(1)}, u32[]{:S(2)}, u32[]{:S(2)}) async-start(bf16[8,32,512]{2,1,0:T(8,128)(2,1)} %bitcast.9), calls=%async_computation.2 | async-start | bytes 524288 | tf_op jit(solution)/shard_map/all_to_all | solution.py:86
  130.8 2.7 %convolution_convert_fusion.10 = bf16[256,256]{1,0:T(8,128)(2,1)S(1)} fusion(bf16[256,3584]{1,0:T(8,128)(2,1)} %copy-done.7), kind=kOutput, calls=%fused_computation.11 | convolution fusion | flops 469827584 | bytes 1966080 | tf_op jit(solution)/shard_map/dot_general | solution.py:278
  134.1 3.7 %all-to-all-done.2 = bf16[8,32,512]{2,1,0:T(8,128)(2,1)S(1)} async-done(((bf16[8,32,512]{2,1,0:T(8,128)(2,1)}), bf16[8,32,512]{2,1,0:T(8,128)(2,1)S(1)}, u32[]{:S(2)}, u32[]{:S(2)}) %all-to-all-start.2) | async-done | bytes 262176 | tf_op jit(solution)/shard_map/all_to_all | solution.py:86
  138.7 3.5 %all-to-all-start.3 = ((bf16[8,64,512]{2,1,0:T(8,128)(2,1)}), bf16[8,64,512]{2,1,0:T(8,128)(2,1)S(1)}, u32[]{:S(2)}, u32[]{:S(2)}) async-start(bf16[8,64,512]{2,1,0:T(8,128)(2,1)} %fusion.6), calls=%async_computation.3 | async-start | bytes 1048576 | tf_op jit(solution)/shard_map/all_to_all | solution.py:98
  142.6 12.8 %all-to-all-done.3 = bf16[8,64,512]{2,1,0:T(8,128)(2,1)S(1)} async-done(((bf16[8,64,512]{2,1,0:T(8,128)(2,1)}), bf16[8,64,512]{2,1,0:T(8,128)(2,1)S(1)}, u32[]{:S(2)}, u32[]{:S(2)}) %all-to-all-start.3) | async-done | bytes 524320 | tf_op jit(solution)/shard_map/all_to_all | solution.py:98
  156.2 1.7 collective-permute-start.24
  157.9 1.3 collective-permute-done.24
  159.6 1.5 collective-permute-start.25
  161.8 2.0 %collective-permute-start.27 = (bf16[192,256]{1,0:T(8,128)(2,1)S(1)}, bf16[192,256]{1,0:T(8,128)(2,1)S(1)}, u32[]{:S(2)}, u32[]{:S(2)}) collective-permute-start(bf16[192,256]{1,0:T(8,128)(2,1)S(1)} %get-tuple-element.48), channel_id=1, source_target_pairs={{0,192},{8,200},{16,208},{24,216},{32,224},{40,232},{48,240},{56,2... | collective-permute-start | bytes 294920 | tf_op jit(solution)/shard_map/ppermute | solution.py:39
  165.2 2.4 %collective-permute-done.26 = bf16[192,256]{1,0:T(8,128)(2,1)S(1)} collective-permute-done((bf16[192,256]{1,0:T(8,128)(2,1)S(1)}, bf16[192,256]{1,0:T(8,128)(2,1)S(1)}, u32[]{:S(2)}, u32[]{:S(2)}) %collective-permute-start.26) | collective-permute-done | bytes 98336 | tf_op jit(solution)/shard_map/ppermute | solution.py:39
  167.7 2.4 %collective-permute-start.28 = (bf16[48,256]{1,0:T(8,128)(2,1)S(1)}, bf16[48,256]{1,0:T(8,128)(2,1)S(1)}, u32[]{:S(2)}, u32[]{:S(2)}) collective-permute-start(bf16[48,256]{1,0:T(8,128)(2,1)S(1)} %get-tuple-element.53), channel_id=1, source_target_pairs={{0,32},{8,40},{16,48},{24,56},{32,0},{40,8},{48,16},{56,24},{64,96... | collective-permute-start | bytes 73736 | tf_op jit(solution)/shard_map/ppermute | solution.py:43
  170.1 1.6 collective-permute-start.29
  171.8 2.0 %collective-permute-start.30 = (bf16[48,256]{1,0:T(8,128)(2,1)S(1)}, bf16[48,256]{1,0:T(8,128)(2,1)S(1)}, u32[]{:S(2)}, u32[]{:S(2)}) collective-permute-start(bf16[48,256]{1,0:T(8,128)(2,1)S(1)} %get-tuple-element.54), channel_id=1, source_target_pairs={{0,48},{8,56},{16,0},{24,8},{32,16},{40,24},{48,32},{56,40},{64,11... | collective-permute-start | bytes 73736 | tf_op jit(solution)/shard_map/ppermute | solution.py:43
  173.7 5.1 %weights.1 = bf16[384,3584]{1,0:T(8,128)(2,1)} custom-call(bf16[384,256]{1,0:T(8,128)(2,1)} %copy-done.4, bf16[256,3584]{1,0:T(8,128)(2,1)} %all-gather.2.cloned.1.call-done.update_ref, bf16[384,3584]{1,0:T(8,128)(2,1)} %weights_ref.1), custom_call_target="tpu_custom_call" | custom-call | flops 704643072 | bytes 8000000 | tf_op jit(solution)/shard_map/weights/pallas_call | solution.py:197
  (113 shorter events, 23.2 us)
Async XLA Ops:
  8.0 12.8 %collective-permute-start = (bf16[48,256]{1,0:T(8,128)(2,1)S(1)}, bf16[48,256]{1,0:T(8,128)(2,1)S(1)}, u32[]{:S(2)}, u32[]{:S(2)}) collective-permute-start(bf16[48,256]{1,0:T(8,128)(2,1)S(1)} %convert_element_type.178), channel_id=1, source_target_pairs={{0,48},{8,56},{16,0},{24,8},{32,16},{40,24},{48,32},{56,40},{64,11... | collective-permute-start | bytes 73736 | tf_op jit(solution)/shard_map/ppermute | solution.py:43
  14.8 6.6 %collective-permute-start.1 = (bf16[48,256]{1,0:T(8,128)(2,1)S(1)}, bf16[48,256]{1,0:T(8,128)(2,1)S(1)}, u32[]{:S(2)}, u32[]{:S(2)}) collective-permute-start(bf16[48,256]{1,0:T(8,128)(2,1)S(1)} %convert_element_type.178), channel_id=1, source_target_pairs={{0,32},{8,40},{16,48},{24,56},{32,0},{40,8},{48,16},{56,24},{64,96... | collective-permute-start | bytes 73736 | tf_op jit(solution)/shard_map/ppermute | solution.py:43
  15.7 5.7 %collective-permute-start.2 = (bf16[48,256]{1,0:T(8,128)(2,1)S(1)}, bf16[48,256]{1,0:T(8,128)(2,1)S(1)}, u32[]{:S(2)}, u32[]{:S(2)}) collective-permute-start(bf16[48,256]{1,0:T(8,128)(2,1)S(1)} %convert_element_type.178), channel_id=1, source_target_pairs={{0,16},{8,24},{16,32},{24,40},{32,48},{40,56},{48,0},{56,8},{64,80... | collective-permute-start | bytes 73736 | tf_op jit(solution)/shard_map/ppermute | solution.py:43
  18.1 1.4 copy-start.2
  21.4 4.5 %collective-permute-start.3 = (bf16[192,256]{1,0:T(8,128)(2,1)S(1)}, bf16[192,256]{1,0:T(8,128)(2,1)S(1)}, u32[]{:S(2)}, u32[]{:S(2)}) collective-permute-start(bf16[192,256]{1,0:T(8,128)(2,1)S(1)} %pad_maximum_fusion.7), channel_id=1, source_target_pairs={{0,192},{8,200},{16,208},{24,216},{32,224},{40,232},{48,240},{56,2... | collective-permute-start | bytes 294920 | tf_op jit(solution)/shard_map/ppermute | solution.py:39
  24.2 5.1 %collective-permute-start.4 = (bf16[192,256]{1,0:T(8,128)(2,1)S(1)}, bf16[192,256]{1,0:T(8,128)(2,1)S(1)}, u32[]{:S(2)}, u32[]{:S(2)}) collective-permute-start(bf16[192,256]{1,0:T(8,128)(2,1)S(1)} %pad_maximum_fusion.7), channel_id=1, source_target_pairs={{0,128},{8,136},{16,144},{24,152},{32,160},{40,168},{48,176},{56,1... | collective-permute-start | bytes 294920 | tf_op jit(solution)/shard_map/ppermute | solution.py:39
  24.6 5.7 %collective-permute-start.5 = (bf16[192,256]{1,0:T(8,128)(2,1)S(1)}, bf16[192,256]{1,0:T(8,128)(2,1)S(1)}, u32[]{:S(2)}, u32[]{:S(2)}) collective-permute-start(bf16[192,256]{1,0:T(8,128)(2,1)S(1)} %pad_maximum_fusion.7), channel_id=1, source_target_pairs={{0,64},{8,72},{16,80},{24,88},{32,96},{40,104},{48,112},{56,120},{... | collective-permute-start | bytes 294920 | tf_op jit(solution)/shard_map/ppermute | solution.py:39
  30.3 5.0 %collective-permute-start.6 = (bf16[768,256]{1,0:T(8,128)(2,1)S(1)}, bf16[768,256]{1,0:T(8,128)(2,1)S(1)}, u32[]{:S(2)}, u32[]{:S(2)}) collective-permute-start(bf16[768,256]{1,0:T(8,128)(2,1)S(1)} %pad_maximum_fusion.1), channel_id=1, source_target_pairs={{0,8},{8,0},{16,24},{24,16},{32,40},{40,32},{48,56},{56,48},{64,72... | collective-permute-start | bytes 1179656 | tf_op jit(solution)/shard_map/ppermute | solution.py:47
  35.3 0.9 copy-start.3
  47.9 9.5 %all-to-all-start.1 = ((bf16[8,32,512]{2,1,0:T(8,128)(2,1)}), bf16[8,32,512]{2,1,0:T(8,128)(2,1)S(1)}, u32[]{:S(2)}, u32[]{:S(2)}) async-start(bf16[8,32,512]{2,1,0:T(8,128)(2,1)} %broadcast_in_dim.19), calls=%async_computation.1 | async-start | bytes 524288 | tf_op jit(solution)/shard_map/all_to_all | solution.py:98
  51.3 122.4 %all-gather.2.cloned.1.call-start = ((), (), s32[]{:S(2)}) async-start(), calls=%async_computation.4 | async-start | bytes 1892352 | tf_op jit(solution)/shard_map/all_gather | solution.py:264
  57.7 2.0 %copy-start = (bf16[512,3584]{1,0:T(8,128)(2,1)S(1)}, bf16[512,3584]{1,0:T(8,128)(2,1)}, u32[]{:S(2)}) copy-start(bf16[512,3584]{1,0:T(8,128)(2,1)} %cot_ref.1) | copy-start | bytes 11010052
  61.8 5.1 %collective-permute-start.7 = (bf16[128,3584]{1,0:T(8,128)(2,1)}, bf16[128,3584]{1,0:T(8,128)(2,1)}, u32[]{:S(2)}, u32[]{:S(2)}) collective-permute-start(bf16[128,3584]{1,0:T(8,128)(2,1)} %get-tuple-element.20), channel_id=1, source_target_pairs={{0,8},{8,0},{16,24},{24,16},{32,40},{40,32},{48,56},{56,48},{64,72... | collective-permute-start | bytes 2752520 | tf_op jit(solution)/shard_map/ppermute | solution.py:47
  68.4 5.5 %collective-permute-start.11 = (bf16[320,256]{1,0:T(8,128)(2,1)S(1)}, bf16[320,256]{1,0:T(8,128)(2,1)S(1)}, u32[]{:S(2)}, u32[]{:S(2)}) collective-permute-start(bf16[320,256]{1,0:T(8,128)(2,1)S(1)} %pad_maximum_fusion.6), channel_id=1, source_target_pairs={{0,1},{1,0},{2,3},{3,2},{4,5},{5,4},{6,7},{7,6},{8,9},{9,8},{10,11... | collective-permute-start | bytes 491528 | tf_op jit(solution)/shard_map/ppermute | solution.py:51
  69.1 6.6 %collective-permute-start.10 = (bf16[32,3584]{1,0:T(8,128)(2,1)S(1)}, bf16[32,3584]{1,0:T(8,128)(2,1)S(1)}, u32[]{:S(2)}, u32[]{:S(2)}) collective-permute-start(bf16[32,3584]{1,0:T(8,128)(2,1)S(1)} %get-tuple-element.43), channel_id=1, source_target_pairs={{0,192},{8,200},{16,208},{24,216},{32,224},{40,232},{48,240},{56,2... | collective-permute-start | bytes 688136 | tf_op jit(solution)/shard_map/ppermute | solution.py:39
  69.5 7.7 %collective-permute-start.8 = (bf16[32,3584]{1,0:T(8,128)(2,1)S(1)}, bf16[32,3584]{1,0:T(8,128)(2,1)S(1)}, u32[]{:S(2)}, u32[]{:S(2)}) collective-permute-start(bf16[32,3584]{1,0:T(8,128)(2,1)S(1)} %get-tuple-element.42), channel_id=1, source_target_pairs={{0,128},{8,136},{16,144},{24,152},{32,160},{40,168},{48,176},{56,1... | collective-permute-start | bytes 688136 | tf_op jit(solution)/shard_map/ppermute | solution.py:39
  70.0 13.4 %collective-permute-start.9 = (bf16[32,3584]{1,0:T(8,128)(2,1)S(1)}, bf16[32,3584]{1,0:T(8,128)(2,1)S(1)}, u32[]{:S(2)}, u32[]{:S(2)}) collective-permute-start(bf16[32,3584]{1,0:T(8,128)(2,1)S(1)} %get-tuple-element.44), channel_id=1, source_target_pairs={{0,64},{8,72},{16,80},{24,88},{32,96},{40,104},{48,112},{56,120},{... | collective-permute-start | bytes 688136 | tf_op jit(solution)/shard_map/ppermute | solution.py:39
  74.0 20.6 %copy-start.5 = (f32[8,3584]{1,0:T(8,128)S(1)}, f32[8,3584]{1,0:T(8,128)}, u32[]{:S(2)}) copy-start(f32[8,3584]{1,0:T(8,128)} %param.10) | copy-start | bytes 344068
  74.0 20.6 %copy-start.6 = (f32[8,3584]{1,0:T(8,128)S(1)}, f32[8,3584]{1,0:T(8,128)}, u32[]{:S(2)}) copy-start(f32[8,3584]{1,0:T(8,128)} %param.11) | copy-start | bytes 344068
  74.0 9.5 %collective-permute-start.12 = (bf16[368,256]{1,0:T(8,128)(2,1)S(1)}, bf16[368,256]{1,0:T(8,128)(2,1)S(1)}, u32[]{:S(2)}, u32[]{:S(2)}) collective-permute-start(bf16[368,256]{1,0:T(8,128)(2,1)S(1)} %pad_maximum_fusion.5), channel_id=1, source_target_pairs={{0,2},{1,3},{2,0},{3,1},{4,6},{5,7},{6,4},{7,5},{8,10},{9,11},{10,... | collective-permute-start | bytes 565256 | tf_op jit(solution)/shard_map/ppermute | solution.py:51
  83.7 7.7 %collective-permute-start.13 = (bf16[8,3584]{1,0:T(8,128)(2,1)S(1)}, bf16[8,3584]{1,0:T(8,128)(2,1)S(1)}, u32[]{:S(2)}, u32[]{:S(2)}) collective-permute-start(bf16[8,3584]{1,0:T(8,128)(2,1)S(1)} %get-tuple-element.50), channel_id=1, source_target_pairs={{0,32},{8,40},{16,48},{24,56},{32,0},{40,8},{48,16},{56,24},{64,96... | collective-permute-start | bytes 172040 | tf_op jit(solution)/shard_map/ppermute | solution.py:43
  87.8 5.5 %collective-permute-start.14 = (bf16[8,3584]{1,0:T(8,128)(2,1)S(1)}, bf16[8,3584]{1,0:T(8,128)(2,1)S(1)}, u32[]{:S(2)}, u32[]{:S(2)}) collective-permute-start(bf16[8,3584]{1,0:T(8,128)(2,1)S(1)} %get-tuple-element.52), channel_id=1, source_target_pairs={{0,16},{8,24},{16,32},{24,40},{32,48},{40,56},{48,0},{56,8},{64,80... | collective-permute-start | bytes 172040 | tf_op jit(solution)/shard_map/ppermute | solution.py:43
  87.8 6.8 %collective-permute-start.15 = (bf16[8,3584]{1,0:T(8,128)(2,1)S(1)}, bf16[8,3584]{1,0:T(8,128)(2,1)S(1)}, u32[]{:S(2)}, u32[]{:S(2)}) collective-permute-start(bf16[8,3584]{1,0:T(8,128)(2,1)S(1)} %get-tuple-element.51), channel_id=1, source_target_pairs={{0,48},{8,56},{16,0},{24,8},{32,16},{40,24},{48,32},{56,40},{64,11... | collective-permute-start | bytes 172040 | tf_op jit(solution)/shard_map/ppermute | solution.py:43
  95.4 7.0 %collective-permute-start.16 = (bf16[8,3584]{1,0:T(8,128)(2,1)S(1)}, bf16[8,3584]{1,0:T(8,128)(2,1)S(1)}, u32[]{:S(2)}, u32[]{:S(2)}) collective-permute-start(bf16[8,3584]{1,0:T(8,128)(2,1)S(1)} %get-tuple-element.35), channel_id=1, source_target_pairs={{0,48},{8,56},{16,0},{24,8},{32,16},{40,24},{48,32},{56,40},{64,11... | collective-permute-start | bytes 172040 | tf_op jit(solution)/shard_map/ppermute | solution.py:43
  97.3 7.1 %collective-permute-start.17 = (bf16[8,3584]{1,0:T(8,128)(2,1)S(1)}, bf16[8,3584]{1,0:T(8,128)(2,1)S(1)}, u32[]{:S(2)}, u32[]{:S(2)}) collective-permute-start(bf16[8,3584]{1,0:T(8,128)(2,1)S(1)} %get-tuple-element.35), channel_id=1, source_target_pairs={{0,32},{8,40},{16,48},{24,56},{32,0},{40,8},{48,16},{56,24},{64,96... | collective-permute-start | bytes 172040 | tf_op jit(solution)/shard_map/ppermute | solution.py:43
  99.1 7.0 %collective-permute-start.18 = (bf16[8,3584]{1,0:T(8,128)(2,1)S(1)}, bf16[8,3584]{1,0:T(8,128)(2,1)S(1)}, u32[]{:S(2)}, u32[]{:S(2)}) collective-permute-start(bf16[8,3584]{1,0:T(8,128)(2,1)S(1)} %get-tuple-element.35), channel_id=1, source_target_pairs={{0,16},{8,24},{16,32},{24,40},{32,48},{40,56},{48,0},{56,8},{64,80... | collective-permute-start | bytes 172040 | tf_op jit(solution)/shard_map/ppermute | solution.py:43
  101.1 6.9 %collective-permute-start.19 = (bf16[464,256]{1,0:T(8,128)(2,1)S(1)}, bf16[464,256]{1,0:T(8,128)(2,1)S(1)}, u32[]{:S(2)}, u32[]{:S(2)}) collective-permute-start(bf16[464,256]{1,0:T(8,128)(2,1)S(1)} %pad_maximum_fusion.2), channel_id=1, source_target_pairs={{0,6},{1,7},{2,4},{3,5},{4,2},{5,3},{6,0},{7,1},{8,14},{9,15},{10,... | collective-permute-start | bytes 712712 | tf_op jit(solution)/shard_map/ppermute | solution.py:51
  108.0 4.9 %collective-permute-start.20 = (bf16[32,3584]{1,0:T(8,128)(2,1)S(1)}, bf16[32,3584]{1,0:T(8,128)(2,1)S(1)}, u32[]{:S(2)}, u32[]{:S(2)}) collective-permute-start(bf16[32,3584]{1,0:T(8,128)(2,1)S(1)} %pad_maximum_fusion.3), channel_id=1, source_target_pairs={{0,192},{8,200},{16,208},{24,216},{32,224},{40,232},{48,240},{56,2... | collective-permute-start | bytes 688136 | tf_op jit(solution)/shard_map/ppermute | solution.py:39
  108.1 6.6 %collective-permute-start.21 = (bf16[32,3584]{1,0:T(8,128)(2,1)S(1)}, bf16[32,3584]{1,0:T(8,128)(2,1)S(1)}, u32[]{:S(2)}, u32[]{:S(2)}) collective-permute-start(bf16[32,3584]{1,0:T(8,128)(2,1)S(1)} %pad_maximum_fusion.3), channel_id=1, source_target_pairs={{0,128},{8,136},{16,144},{24,152},{32,160},{40,168},{48,176},{56,1... | collective-permute-start | bytes 688136 | tf_op jit(solution)/shard_map/ppermute | solution.py:39
  108.7 12.6 %collective-permute-start.22 = (bf16[32,3584]{1,0:T(8,128)(2,1)S(1)}, bf16[32,3584]{1,0:T(8,128)(2,1)S(1)}, u32[]{:S(2)}, u32[]{:S(2)}) collective-permute-start(bf16[32,3584]{1,0:T(8,128)(2,1)S(1)} %pad_maximum_fusion.3), channel_id=1, source_target_pairs={{0,64},{8,72},{16,80},{24,88},{32,96},{40,104},{48,112},{56,120},{... | collective-permute-start | bytes 688136 | tf_op jit(solution)/shard_map/ppermute | solution.py:39
  109.9 23.7 %copy-start.4 = (bf16[384,256]{1,0:T(8,128)(2,1)}, bf16[384,256]{1,0:T(8,128)(2,1)S(1)}, u32[]{:S(2)}) copy-start(bf16[384,256]{1,0:T(8,128)(2,1)S(1)} %convolution_convert_fusion.7.proj_ref) | copy-start | bytes 589828
  121.3 4.1 %copy-start.1 = (bf16[512,3584]{1,0:T(8,128)(2,1)S(1)}, bf16[512,3584]{1,0:T(8,128)(2,1)}, u32[]{:S(2)}) copy-start(bf16[512,3584]{1,0:T(8,128)(2,1)} %cot_ref.1) | copy-start | bytes 11010052
  121.4 4.0 %collective-permute-start.23 = (bf16[128,3584]{1,0:T(8,128)(2,1)S(1)}, bf16[128,3584]{1,0:T(8,128)(2,1)S(1)}, u32[]{:S(2)}, u32[]{:S(2)}) collective-permute-start(bf16[128,3584]{1,0:T(8,128)(2,1)S(1)} %pad_maximum_fusion), channel_id=1, source_target_pairs={{0,8},{8,0},{16,24},{24,16},{32,40},{40,32},{48,56},{56,48},{64,72... | collective-permute-start | bytes 2752520 | tf_op jit(solution)/shard_map/ppermute | solution.py:47
  125.5 1.9 %copy-start.7 = (bf16[256,3584]{1,0:T(8,128)(2,1)}, bf16[256,3584]{1,0:T(8,128)(2,1)S(1)}, u32[]{:S(2)}) copy-start(bf16[256,3584]{1,0:T(8,128)(2,1)S(1)} %constant_dynamic-update-slice_fusion.5) | copy-start | bytes 5505028
  127.4 10.4 %all-to-all-start.2 = ((bf16[8,32,512]{2,1,0:T(8,128)(2,1)}), bf16[8,32,512]{2,1,0:T(8,128)(2,1)S(1)}, u32[]{:S(2)}, u32[]{:S(2)}) async-start(bf16[8,32,512]{2,1,0:T(8,128)(2,1)} %bitcast.9), calls=%async_computation.2 | async-start | bytes 524288 | tf_op jit(solution)/shard_map/all_to_all | solution.py:86
  138.7 16.7 %all-to-all-start.3 = ((bf16[8,64,512]{2,1,0:T(8,128)(2,1)}), bf16[8,64,512]{2,1,0:T(8,128)(2,1)S(1)}, u32[]{:S(2)}, u32[]{:S(2)}) async-start(bf16[8,64,512]{2,1,0:T(8,128)(2,1)} %fusion.6), calls=%async_computation.3 | async-start | bytes 1048576 | tf_op jit(solution)/shard_map/all_to_all | solution.py:98
  156.2 3.0 %collective-permute-start.24 = (bf16[768,256]{1,0:T(8,128)(2,1)S(1)}, bf16[768,256]{1,0:T(8,128)(2,1)S(1)}, u32[]{:S(2)}, u32[]{:S(2)}) collective-permute-start(bf16[768,256]{1,0:T(8,128)(2,1)S(1)} %convolution_convert_fusion), channel_id=1, source_target_pairs={{0,8},{8,0},{16,24},{24,16},{32,40},{40,32},{48,56},{56,48},{64,72... | collective-permute-start | bytes 1179656 | tf_op jit(solution)/shard_map/ppermute | solution.py:47
  159.6 5.6 %collective-permute-start.25 = (bf16[192,256]{1,0:T(8,128)(2,1)S(1)}, bf16[192,256]{1,0:T(8,128)(2,1)S(1)}, u32[]{:S(2)}, u32[]{:S(2)}) collective-permute-start(bf16[192,256]{1,0:T(8,128)(2,1)S(1)} %get-tuple-element.47), channel_id=1, source_target_pairs={{0,128},{8,136},{16,144},{24,152},{32,160},{40,168},{48,176},{56,1... | collective-permute-start | bytes 294920 | tf_op jit(solution)/shard_map/ppermute | solution.py:39
  161.1 6.5 %collective-permute-start.26 = (bf16[192,256]{1,0:T(8,128)(2,1)S(1)}, bf16[192,256]{1,0:T(8,128)(2,1)S(1)}, u32[]{:S(2)}, u32[]{:S(2)}) collective-permute-start(bf16[192,256]{1,0:T(8,128)(2,1)S(1)} %get-tuple-element.49), channel_id=1, source_target_pairs={{0,64},{8,72},{16,80},{24,88},{32,96},{40,104},{48,112},{56,120},{... | collective-permute-start | bytes 294920 | tf_op jit(solution)/shard_map/ppermute | solution.py:39
  161.8 5.8 %collective-permute-start.27 = (bf16[192,256]{1,0:T(8,128)(2,1)S(1)}, bf16[192,256]{1,0:T(8,128)(2,1)S(1)}, u32[]{:S(2)}, u32[]{:S(2)}) collective-permute-start(bf16[192,256]{1,0:T(8,128)(2,1)S(1)} %get-tuple-element.48), channel_id=1, source_target_pairs={{0,192},{8,200},{16,208},{24,216},{32,224},{40,232},{48,240},{56,2... | collective-permute-start | bytes 294920 | tf_op jit(solution)/shard_map/ppermute | solution.py:39
  167.7 11.1 %collective-permute-start.28 = (bf16[48,256]{1,0:T(8,128)(2,1)S(1)}, bf16[48,256]{1,0:T(8,128)(2,1)S(1)}, u32[]{:S(2)}, u32[]{:S(2)}) collective-permute-start(bf16[48,256]{1,0:T(8,128)(2,1)S(1)} %get-tuple-element.53), channel_id=1, source_target_pairs={{0,32},{8,40},{16,48},{24,56},{32,0},{40,8},{48,16},{56,24},{64,96... | collective-permute-start | bytes 73736 | tf_op jit(solution)/shard_map/ppermute | solution.py:43
  170.1 8.6 %collective-permute-start.29 = (bf16[48,256]{1,0:T(8,128)(2,1)S(1)}, bf16[48,256]{1,0:T(8,128)(2,1)S(1)}, u32[]{:S(2)}, u32[]{:S(2)}) collective-permute-start(bf16[48,256]{1,0:T(8,128)(2,1)S(1)} %get-tuple-element.55), channel_id=1, source_target_pairs={{0,16},{8,24},{16,32},{24,40},{32,48},{40,56},{48,0},{56,8},{64,80... | collective-permute-start | bytes 73736 | tf_op jit(solution)/shard_map/ppermute | solution.py:43
  171.8 7.0 %collective-permute-start.30 = (bf16[48,256]{1,0:T(8,128)(2,1)S(1)}, bf16[48,256]{1,0:T(8,128)(2,1)S(1)}, u32[]{:S(2)}, u32[]{:S(2)}) collective-permute-start(bf16[48,256]{1,0:T(8,128)(2,1)S(1)} %get-tuple-element.54), channel_id=1, source_target_pairs={{0,48},{8,56},{16,0},{24,8},{32,16},{40,24},{48,32},{56,40},{64,11... | collective-permute-start | bytes 73736 | tf_op jit(solution)/shard_map/ppermute | solution.py:43
Sparse Core Ops, SparseCore 0:
  102.5 53.4 all-gather.1

commit v3 on v2

--- a/solution.py
+++ b/solution.py
@@ -69,35 +69,40 @@
     return high, (value - high.astype(f32)).astype(bf16)
 
 
-def side_step(gram, rows, mask):
+def side_step(gram, rows, mask, trigger=None):
     n = gram.shape[0]
     eye = jnp.eye(n, dtype=f32)
     high, low = split_high(gram)
     rest = jnp.sum(low.astype(f32) * eye, axis=0).astype(bf16)
     payload = jnp.concatenate([high, jnp.broadcast_to(rest, (16, n)), rows], axis=0)
+    if trigger is not None:
+        payload = after(payload, trigger)
     got = send_xor(payload, mask)
     gram = gram + got[:n].astype(f32) + eye * got[n : n + 1].astype(f32)
     return gram, jnp.concatenate([rows, got[n + 16 :]], axis=0)
 
 
-def split_sum(part):
+def split_sum(part, extra=None):
     n = NX * NL
     rows, cols = part.shape
-    got = lax.all_to_all(part.astype(bf16).reshape(n, rows // n, cols), "tensor", 0, 0)
-    return jnp.sum(got.astype(f32), axis=0).astype(bf16)
-
-
-def spread(own, extra=None):
+    share = rows // n
+    blocks = part.astype(bf16).reshape(n, share, cols)
+    if extra is not None:
+        high, wide = extra.shape
+        extra = jnp.pad(extra.astype(bf16), ((0, 16 - high), (0, cols - wide)))
+        blocks = jnp.concatenate([blocks, jnp.broadcast_to(extra, (n, 16, cols))], axis=1)
+    got = lax.all_to_all(blocks, "tensor", 0, 0)
+    own = jnp.sum(got[:, :share].astype(f32), axis=0).astype(bf16)
+    if extra is None:
+        return own
+    return own, jnp.sum(got[:, share : share + high, :wide].astype(f32), axis=0)
+
+
+def spread(own):
     n = NX * NL
     rows, cols = own.shape
     blocks = jnp.broadcast_to(own, (n, rows, cols))
-    if extra is not None:
-        extra_rows = extra.shape[1]
-        extra = jnp.pad(extra, ((0, 0), (0, rows - extra_rows), (0, 0)))
-        blocks = jnp.concatenate([blocks, extra], axis=1)
-    got = lax.all_to_all(blocks, "tensor", 0, 0)
-    whole = got[:, :rows].reshape(n * rows, cols)
-    return whole if extra is None else (whole, got[:, rows : rows + extra_rows])
+    return lax.all_to_all(blocks, "tensor", 0, 0).reshape(n * rows, cols)
 
 
 def reduce_blocks(rows, send, beside=None):
@@ -250,12 +255,9 @@
 
     grad_keep, grad_send = gradient_parts(latent_p, out_grads)
     total = grad_keep + send_core(grad_send).astype(f32)
-    side = after((gram_part, proj_half), total)
-    total = reduce_ring(total, send_y)
-    for mask in (1, 2):
-        side = side_step(*side, mask)
-    total, *side = lax.optimization_barrier((total, *side))
-    gradient, first_got = reduce_blocks(total, send_z)
+    side = side_step(*side_step(gram_part, proj_half, 1, total), 2)
+    total, *side = lax.optimization_barrier((reduce_ring(total, send_y), *side))
+    gradient = reduce_ring(total, send_z)
     grad_half = gradient.astype(bf16)
     new_first, new_second, update = adam_rows(gradient, moment_first, moment_second)
     grad_own = gather_ring(grad_half, send_z)
@@ -270,14 +272,9 @@
     proj_block = jnp.dot(
         one_hot(place, place_q), proj_rows, preferred_element_type=f32
     ).astype(bf16)
-    proj_block_p = lax.dot_general(
-        proj_block, p_from_r, NT, preferred_element_type=f32
-    ).astype(bf16)
-
-    token_own = split_sum(lax.dot_general(grad_p, out_grads, NT, preferred_element_type=f32))
-    gram_k = lax.dot_general(grad_p, grad_p, NT, preferred_element_type=f32).astype(bf16)
-    second_part = jnp.dot(proj_block_p, gram_k, preferred_element_type=f32).astype(bf16)
-    token_p, second = spread(token_own, second_part.reshape(NX * NL, -1, tokens))
+
+    token_part = lax.dot_general(grad_p, out_grads, NT, preferred_element_type=f32)
+    gram_rows = lax.dot_general(grad_half, grad_p, NT, preferred_element_type=f32)
     mix = 4.0 * jnp.eye(ranks, dtype=f32) - 2.0 * gram_q
     mix_p = jnp.concatenate(
         [
@@ -286,21 +283,30 @@
         ],
         axis=0,
     )
+    token_own, gram_rows = split_sum(token_part, gram_rows)
+    token_own, proj_block = lax.optimization_barrier((token_own, proj_block))
+    token_p = spread(token_own)
+    own_rank = lax.axis_index("dp") * 8 + jnp.arange(8, dtype=jnp.int32)
+    gram_rows = jnp.dot((-2.0 * gram_rows).astype(bf16), p_from_r, preferred_element_type=f32)
+    gram_place = jnp.dot(
+        one_hot(rank, own_rank), gram_rows.astype(bf16), preferred_element_type=f32
+    ).astype(bf16)
     token_r = lax.dot_general(
         mix_p, jnp.concatenate([token_p, token_p], axis=0), TN, preferred_element_type=f32
     ).astype(bf16)
 
     n = x_rel.shape[0] // 2
-    feat_send = lax.dot_general(x_rel[n:], token_r, NT, preferred_element_type=f32)
-    feat_keep = lax.dot_general(x_rel[:n], token_r, NT, preferred_element_type=f32)
+    feat_send, feat_keep = [
+        lax.dot_general(x_rel[part], token_r, NT, preferred_element_type=f32)
+        + jnp.dot(proj_rel[part], gram_place, preferred_element_type=f32)
+        for part in (slice(n, None), slice(0, n))
+    ]
     total = feat_keep + send_core(feat_send.astype(bf16)).astype(f32)
     total = reduce_ring(total, send_y)
     new_weights = weights_step(proj_block, update_all, weights)
     feature_sum = reduce_blocks(total, send_z, new_weights)[0]
 
-    second = jnp.sum(second.astype(f32), axis=0).reshape(block_width, ranks)
-    second = jnp.dot(second, p_from_r.astype(f32), precision=HIGHEST)
-    increment = proj_rate * (feature_sum - 2.0 * second)
+    increment = proj_rate * feature_sum
     return (new_weights, new_first, new_second, increment)
 
 

time: 187 us -> 186 us (level)
  matrix products: 9.77 us -> 7.82 us
    dot_general x5 -> x6, matrix products: 4.26 us -> 2.28 us  [the longest x2 0.79 us: body(): lax.dot_general(x_rel[part], token_r, NT, preferred_element_type=f32)]
    unnamed x24 -> x27, local copies, waits for them, and re-layouts: 3.86 us -> 4.63 us
  transfers between devices with their start and end apart: 35 -> 35, of which waited for: 25 -> 25; matrix products, arithmetic and copies ran while one was open for 6% -> 5% of each run, Pallas kernels for 3% -> 3%
where the time goes in v3:
time: 186 us; the launch traced here: 185 us
  waiting for transfers between devices  69.1 us (37%)
  starting transfers between devices  62.7 us (34%)
  between operations  14.5 us (8%)
  blocking collectives  11 us (6%)
  Pallas kernels  8.27 us (4%)
  matrix products  7.82 us (4%)
  local copies, waits for them, and re-layouts  6.35 us (3%)
  other arithmetic  5.18 us (3%)
    ppermute x12, waiting for transfers between devices, send_y(): return lax.ppermute(block, 'dp', dp_pairs(k, 0, 0))  29.6 us
    ppermute x12, starting transfers between devices, send_z(): return lax.ppermute(block, 'dp', dp_pairs(0, k, 0))  29.3 us
    all_to_all x2, waiting for transfers between devices, spread(): return lax.all_to_all(blocks, 'tensor', 0, 0).reshape(n * rows, cols)  15.1 us
    ppermute x12, starting transfers between devices, send_y(): return lax.ppermute(block, 'dp', dp_pairs(k, 0, 0))  11.4 us
    all_to_all x1, blocking collectives, split_sum(): got = lax.all_to_all(blocks, 'tensor', 0, 0)  11 us
    ppermute x4, starting transfers between devices, send_core(): return lax.ppermute(block, 'dp', dp_pairs(0, 0, 1))  9.61 us
    ppermute x12, waiting for transfers between devices, send_z(): return lax.ppermute(block, 'dp', dp_pairs(0, k, 0))  7.55 us
    all_to_all x1, waiting for transfers between devices, split_sum(): got = lax.all_to_all(blocks, 'tensor', 0, 0)  6.91 us
  transfers between devices with their start and end apart: 35, of which 25 were waited for; matrix products, arithmetic and copies ran while one was open for 5% of the time, Pallas kernels for 3%

profile of v3, /device:TPU:1, one launch (start us, length us, event | category | flops | bytes accessed | tf_op | source)
XLA Modules:
  0.0 184.8 jit_solution(6553068328008066782)
XLA Ops:
  8.0 6.8 %collective-permute-start = (bf16[48,256]{1,0:T(8,128)(2,1)S(1)}, bf16[48,256]{1,0:T(8,128)(2,1)S(1)}, u32[]{:S(2)}, u32[]{:S(2)}) collective-permute-start(bf16[48,256]{1,0:T(8,128)(2,1)S(1)} %convert_element_type.181), channel_id=1, source_target_pairs={{0,48},{8,56},{16,0},{24,8},{32,16},{40,24},{48,32},{56,40},{64,11... | collective-permute-start | bytes 73736 | tf_op jit(solution)/shard_map/ppermute | solution.py:43
  15.7 2.4 %collective-permute-start.2 = (bf16[48,256]{1,0:T(8,128)(2,1)S(1)}, bf16[48,256]{1,0:T(8,128)(2,1)S(1)}, u32[]{:S(2)}, u32[]{:S(2)}) collective-permute-start(bf16[48,256]{1,0:T(8,128)(2,1)S(1)} %convert_element_type.181), channel_id=1, source_target_pairs={{0,16},{8,24},{16,32},{24,40},{32,48},{40,56},{48,0},{56,8},{64,80... | collective-permute-start | bytes 73736 | tf_op jit(solution)/shard_map/ppermute | solution.py:43
  18.2 1.4 copy-done.2
  21.4 2.8 %collective-permute-start.3 = (bf16[192,256]{1,0:T(8,128)(2,1)S(1)}, bf16[192,256]{1,0:T(8,128)(2,1)S(1)}, u32[]{:S(2)}, u32[]{:S(2)}) collective-permute-start(bf16[192,256]{1,0:T(8,128)(2,1)S(1)} %fusion.29), channel_id=1, source_target_pairs={{0,192},{8,200},{16,208},{24,216},{32,224},{40,232},{48,240},{56,2... | collective-permute-start | bytes 294920 | tf_op jit(solution)/shard_map/ppermute | solution.py:39
  25.9 3.4 %collective-permute-done.4 = bf16[192,256]{1,0:T(8,128)(2,1)S(1)} collective-permute-done((bf16[192,256]{1,0:T(8,128)(2,1)S(1)}, bf16[192,256]{1,0:T(8,128)(2,1)S(1)}, u32[]{:S(2)}, u32[]{:S(2)}) %collective-permute-start.4) | collective-permute-done | bytes 98336 | tf_op jit(solution)/shard_map/ppermute | solution.py:39
  30.3 3.6 %collective-permute-start.6 = (bf16[768,256]{1,0:T(8,128)(2,1)S(1)}, bf16[768,256]{1,0:T(8,128)(2,1)S(1)}, u32[]{:S(2)}, u32[]{:S(2)}) collective-permute-start(bf16[768,256]{1,0:T(8,128)(2,1)S(1)} %get-tuple-element.58), channel_id=1, source_target_pairs={{0,8},{8,0},{16,24},{24,16},{32,40},{40,32},{48,56},{56,48},{64,72... | collective-permute-start | bytes 1179656 | tf_op jit(solution)/shard_map/ppermute | solution.py:47
  33.9 1.3 collective-permute-done.6
  36.9 11.0 %all_to_all.20 = bf16[8,32,512]{2,1,0:T(8,128)(2,1)S(1)} all-to-all(bf16[8,32,512]{2,1,0:T(8,128)(2,1)S(1)} %bitcast.28), channel_id=1, replica_groups=mesh['dp'=32,'tensor'=8] {'tensor'}, dimensions={0} | all-to-all | bytes 524288 | tf_op jit(solution)/shard_map/all_to_all | solution.py:94
  48.7 3.4 %all-to-all-start.1 = ((bf16[8,32,512]{2,1,0:T(8,128)(2,1)}), bf16[8,32,512]{2,1,0:T(8,128)(2,1)S(1)}, u32[]{:S(2)}, u32[]{:S(2)}) async-start(bf16[8,32,512]{2,1,0:T(8,128)(2,1)} %broadcast_in_dim.24), calls=%async_computation.1 | async-start | bytes 524288 | tf_op jit(solution)/shard_map/all_to_all | solution.py:105
  52.2 6.0 %all-to-all-done.1 = bf16[8,32,512]{2,1,0:T(8,128)(2,1)S(1)} async-done(((bf16[8,32,512]{2,1,0:T(8,128)(2,1)}), bf16[8,32,512]{2,1,0:T(8,128)(2,1)S(1)}, u32[]{:S(2)}, u32[]{:S(2)}) %all-to-all-start.1) | async-done | bytes 262176 | tf_op jit(solution)/shard_map/all_to_all | solution.py:105
  58.5 2.0 %copy-done = bf16[512,3584]{1,0:T(8,128)(2,1)S(1)} copy-done((bf16[512,3584]{1,0:T(8,128)(2,1)S(1)}, bf16[512,3584]{1,0:T(8,128)(2,1)}, u32[]{:S(2)}) %copy-start) | copy-done | bytes 3670040
  60.5 2.0 %gradient.1 = (f32[128,3584]{1,0:T(8,128)S(1)}, bf16[128,3584]{1,0:T(8,128)(2,1)}) custom-call(bf16[256,512]{1,0:T(8,128)(2,1)S(1)} %convolution_convert_fusion.2.latent_ref, bf16[512,3584]{1,0:T(8,128)(2,1)S(1)} %copy-done), custom_call_target="tpu_custom_call" | custom-call | flops 939524096 | bytes 6500000 | tf_op jit(solution)/shard_map/gradient/pallas_call | solution.py:177
  62.6 2.6 %collective-permute-start.7 = (bf16[128,3584]{1,0:T(8,128)(2,1)}, bf16[128,3584]{1,0:T(8,128)(2,1)}, u32[]{:S(2)}, u32[]{:S(2)}) collective-permute-start(bf16[128,3584]{1,0:T(8,128)(2,1)} %get-tuple-element.21), channel_id=1, source_target_pairs={{0,8},{8,0},{16,24},{24,16},{32,40},{40,32},{48,56},{56,48},{64,72... | collective-permute-start | bytes 2752520 | tf_op jit(solution)/shard_map/ppermute | solution.py:47
  65.2 1.8 select_reduce_fusion.2
  67.6 1.4 fusion.69
  71.4 3.2 %collective-permute-done.11 = bf16[320,256]{1,0:T(8,128)(2,1)S(1)} collective-permute-done((bf16[320,256]{1,0:T(8,128)(2,1)S(1)}, bf16[320,256]{1,0:T(8,128)(2,1)S(1)}, u32[]{:S(2)}, u32[]{:S(2)}) %collective-permute-start.11) | collective-permute-done | bytes 163872 | tf_op jit(solution)/shard_map/ppermute | solution.py:51
  74.8 1.5 collective-permute-done.10
  76.3 1.5 collective-permute-done.8
  77.9 6.2 %collective-permute-done.9 = bf16[32,3584]{1,0:T(8,128)(2,1)S(1)} collective-permute-done((bf16[32,3584]{1,0:T(8,128)(2,1)S(1)}, bf16[32,3584]{1,0:T(8,128)(2,1)S(1)}, u32[]{:S(2)}, u32[]{:S(2)}) %collective-permute-start.9) | collective-permute-done | bytes 229408 | tf_op jit(solution)/shard_map/ppermute | solution.py:39
  84.4 4.1 %collective-permute-start.13 = (bf16[8,3584]{1,0:T(8,128)(2,1)S(1)}, bf16[8,3584]{1,0:T(8,128)(2,1)S(1)}, u32[]{:S(2)}, u32[]{:S(2)}) collective-permute-start(bf16[8,3584]{1,0:T(8,128)(2,1)S(1)} %get-tuple-element.52), channel_id=1, source_target_pairs={{0,32},{8,40},{16,48},{24,56},{32,0},{40,8},{48,16},{56,24},{64,96... | collective-permute-start | bytes 172040 | tf_op jit(solution)/shard_map/ppermute | solution.py:43
  88.5 3.6 %collective-permute-start.15 = (bf16[8,3584]{1,0:T(8,128)(2,1)S(1)}, bf16[8,3584]{1,0:T(8,128)(2,1)S(1)}, u32[]{:S(2)}, u32[]{:S(2)}) collective-permute-start(bf16[8,3584]{1,0:T(8,128)(2,1)S(1)} %get-tuple-element.53), channel_id=1, source_target_pairs={{0,48},{8,56},{16,0},{24,8},{32,16},{40,24},{48,32},{56,40},{64,11... | collective-permute-start | bytes 172040 | tf_op jit(solution)/shard_map/ppermute | solution.py:43
  92.1 1.9 %collective-permute-done.14 = bf16[8,3584]{1,0:T(8,128)(2,1)S(1)} collective-permute-done((bf16[8,3584]{1,0:T(8,128)(2,1)S(1)}, bf16[8,3584]{1,0:T(8,128)(2,1)S(1)}, u32[]{:S(2)}, u32[]{:S(2)}) %collective-permute-start.14) | collective-permute-done | bytes 57376 | tf_op jit(solution)/shard_map/ppermute | solution.py:43
  94.0 1.3 collective-permute-done.15
  96.1 1.9 %collective-permute-start.16 = (bf16[8,3584]{1,0:T(8,128)(2,1)S(1)}, bf16[8,3584]{1,0:T(8,128)(2,1)S(1)}, u32[]{:S(2)}, u32[]{:S(2)}) collective-permute-start(bf16[8,3584]{1,0:T(8,128)(2,1)S(1)} %get-tuple-element.37), channel_id=1, source_target_pairs={{0,48},{8,56},{16,0},{24,8},{32,16},{40,24},{48,32},{56,40},{64,11... | collective-permute-start | bytes 172040 | tf_op jit(solution)/shard_map/ppermute | solution.py:43
  98.0 1.8 collective-permute-start.17
  99.8 1.9 %collective-permute-start.18 = (bf16[8,3584]{1,0:T(8,128)(2,1)S(1)}, bf16[8,3584]{1,0:T(8,128)(2,1)S(1)}, u32[]{:S(2)}, u32[]{:S(2)}) collective-permute-start(bf16[8,3584]{1,0:T(8,128)(2,1)S(1)} %get-tuple-element.37), channel_id=1, source_target_pairs={{0,16},{8,24},{16,32},{24,40},{32,48},{40,56},{48,0},{56,8},{64,80... | collective-permute-start | bytes 172040 | tf_op jit(solution)/shard_map/ppermute | solution.py:43
  101.7 1.3 collective-permute-start.19
  103.1 2.0 %collective-permute-done.17 = bf16[8,3584]{1,0:T(8,128)(2,1)S(1)} collective-permute-done((bf16[8,3584]{1,0:T(8,128)(2,1)S(1)}, bf16[8,3584]{1,0:T(8,128)(2,1)S(1)}, u32[]{:S(2)}, u32[]{:S(2)}) %collective-permute-start.17) | collective-permute-done | bytes 57376 | tf_op jit(solution)/shard_map/ppermute | solution.py:43
  105.1 1.6 collective-permute-done.18
  106.8 1.8 collective-permute-done.19
  110.2 3.4 %collective-permute-done.20 = bf16[32,3584]{1,0:T(8,128)(2,1)S(1)} collective-permute-done((bf16[32,3584]{1,0:T(8,128)(2,1)S(1)}, bf16[32,3584]{1,0:T(8,128)(2,1)S(1)}, u32[]{:S(2)}, u32[]{:S(2)}) %collective-permute-start.20) | collective-permute-done | bytes 229408 | tf_op jit(solution)/shard_map/ppermute | solution.py:39
  113.6 1.7 collective-permute-done.21
  115.3 6.7 %collective-permute-done.22 = bf16[32,3584]{1,0:T(8,128)(2,1)S(1)} collective-permute-done((bf16[32,3584]{1,0:T(8,128)(2,1)S(1)}, bf16[32,3584]{1,0:T(8,128)(2,1)S(1)}, u32[]{:S(2)}, u32[]{:S(2)}) %collective-permute-start.22) | collective-permute-done | bytes 229408 | tf_op jit(solution)/shard_map/ppermute | solution.py:39
  122.1 1.9 %collective-permute-start.23 = (bf16[128,3584]{1,0:T(8,128)(2,1)S(1)}, bf16[128,3584]{1,0:T(8,128)(2,1)S(1)}, u32[]{:S(2)}, u32[]{:S(2)}) collective-permute-start(bf16[128,3584]{1,0:T(8,128)(2,1)S(1)} %pad_maximum_fusion), channel_id=1, source_target_pairs={{0,8},{8,0},{16,24},{24,16},{32,40},{40,32},{48,56},{56,48},{64,72... | collective-permute-start | bytes 2752520 | tf_op jit(solution)/shard_map/ppermute | solution.py:47
  124.1 2.0 %collective-permute-done.23 = bf16[128,3584]{1,0:T(8,128)(2,1)S(1)} collective-permute-done((bf16[128,3584]{1,0:T(8,128)(2,1)S(1)}, bf16[128,3584]{1,0:T(8,128)(2,1)S(1)}, u32[]{:S(2)}, u32[]{:S(2)}) %collective-permute-start.23) | collective-permute-done | bytes 917536 | tf_op jit(solution)/shard_map/ppermute | solution.py:47
  128.7 3.5 %all-to-all-start.2 = ((bf16[8,48,512]{2,1,0:T(8,128)(2,1)}), bf16[8,48,512]{2,1,0:T(8,128)(2,1)S(1)}, u32[]{:S(2)}, u32[]{:S(2)}) async-start(bf16[8,48,512]{2,1,0:T(8,128)(2,1)} %pad_maximum_fusion.1), calls=%async_computation.2 | async-start | bytes 786432 | tf_op jit(solution)/shard_map/all_to_all | solution.py:94
  133.4 6.9 %all-to-all-done.2 = bf16[8,48,512]{2,1,0:T(8,128)(2,1)S(1)} async-done(((bf16[8,48,512]{2,1,0:T(8,128)(2,1)}), bf16[8,48,512]{2,1,0:T(8,128)(2,1)S(1)}, u32[]{:S(2)}, u32[]{:S(2)}) %all-to-all-start.2) | async-done | bytes 393248 | tf_op jit(solution)/shard_map/all_to_all | solution.py:94
  141.1 3.4 %all-to-all-start.3 = ((bf16[8,32,512]{2,1,0:T(8,128)(2,1)}), bf16[8,32,512]{2,1,0:T(8,128)(2,1)S(1)}, u32[]{:S(2)}, u32[]{:S(2)}) async-start(bf16[8,32,512]{2,1,0:T(8,128)(2,1)} %broadcast_in_dim.29), calls=%async_computation.3 | async-start | bytes 524288 | tf_op jit(solution)/shard_map/all_to_all | solution.py:105
  145.2 9.1 %all-to-all-done.3 = bf16[8,32,512]{2,1,0:T(8,128)(2,1)S(1)} async-done(((bf16[8,32,512]{2,1,0:T(8,128)(2,1)}), bf16[8,32,512]{2,1,0:T(8,128)(2,1)S(1)}, u32[]{:S(2)}, u32[]{:S(2)}) %all-to-all-start.3) | async-done | bytes 262176 | tf_op jit(solution)/shard_map/all_to_all | solution.py:105
  155.2 1.4 collective-permute-start.24
  158.3 1.7 collective-permute-start.25
  160.7 2.0 %collective-permute-start.27 = (bf16[192,256]{1,0:T(8,128)(2,1)S(1)}, bf16[192,256]{1,0:T(8,128)(2,1)S(1)}, u32[]{:S(2)}, u32[]{:S(2)}) collective-permute-start(bf16[192,256]{1,0:T(8,128)(2,1)S(1)} %get-tuple-element.50), channel_id=1, source_target_pairs={{0,192},{8,200},{16,208},{24,216},{32,224},{40,232},{48,240},{56,2... | collective-permute-start | bytes 294920 | tf_op jit(solution)/shard_map/ppermute | solution.py:39
  162.7 1.3 collective-permute-done.25
  163.9 2.4 %collective-permute-done.26 = bf16[192,256]{1,0:T(8,128)(2,1)S(1)} collective-permute-done((bf16[192,256]{1,0:T(8,128)(2,1)S(1)}, bf16[192,256]{1,0:T(8,128)(2,1)S(1)}, u32[]{:S(2)}, u32[]{:S(2)}) %collective-permute-start.26) | collective-permute-done | bytes 98336 | tf_op jit(solution)/shard_map/ppermute | solution.py:39
  166.4 2.3 %collective-permute-start.28 = (bf16[48,256]{1,0:T(8,128)(2,1)S(1)}, bf16[48,256]{1,0:T(8,128)(2,1)S(1)}, u32[]{:S(2)}, u32[]{:S(2)}) collective-permute-start(bf16[48,256]{1,0:T(8,128)(2,1)S(1)} %get-tuple-element.55), channel_id=1, source_target_pairs={{0,32},{8,40},{16,48},{24,56},{32,0},{40,8},{48,16},{56,24},{64,96... | collective-permute-start | bytes 73736 | tf_op jit(solution)/shard_map/ppermute | solution.py:43
  168.7 1.2 collective-permute-start.29
  169.9 2.4 %collective-permute-start.30 = (bf16[48,256]{1,0:T(8,128)(2,1)S(1)}, bf16[48,256]{1,0:T(8,128)(2,1)S(1)}, u32[]{:S(2)}, u32[]{:S(2)}) collective-permute-start(bf16[48,256]{1,0:T(8,128)(2,1)S(1)} %get-tuple-element.56), channel_id=1, source_target_pairs={{0,48},{8,56},{16,0},{24,8},{32,16},{40,24},{48,32},{56,40},{64,11... | collective-permute-start | bytes 73736 | tf_op jit(solution)/shard_map/ppermute | solution.py:43
  172.3 5.1 %weights.1 = bf16[384,3584]{1,0:T(8,128)(2,1)} custom-call(bf16[384,256]{1,0:T(8,128)(2,1)} %convolution_convert_fusion.4.proj_ref, bf16[256,3584]{1,0:T(8,128)(2,1)} %all-gather.2.cloned.1.call-done.update_ref, bf16[384,3584]{1,0:T(8,128)(2,1)} %weights_ref.1), custom_call_target="tpu_custom_call" | custom-call | flops 704643072 | bytes 8000000 | tf_op jit(solution)/shard_map/weights/pallas_call | solution.py:202
  (116 shorter events, 24.2 us)
Async XLA Ops:
  8.0 12.8 %collective-permute-start = (bf16[48,256]{1,0:T(8,128)(2,1)S(1)}, bf16[48,256]{1,0:T(8,128)(2,1)S(1)}, u32[]{:S(2)}, u32[]{:S(2)}) collective-permute-start(bf16[48,256]{1,0:T(8,128)(2,1)S(1)} %convert_element_type.181), channel_id=1, source_target_pairs={{0,48},{8,56},{16,0},{24,8},{32,16},{40,24},{48,32},{56,40},{64,11... | collective-permute-start | bytes 73736 | tf_op jit(solution)/shard_map/ppermute | solution.py:43
  14.8 6.6 %collective-permute-start.1 = (bf16[48,256]{1,0:T(8,128)(2,1)S(1)}, bf16[48,256]{1,0:T(8,128)(2,1)S(1)}, u32[]{:S(2)}, u32[]{:S(2)}) collective-permute-start(bf16[48,256]{1,0:T(8,128)(2,1)S(1)} %convert_element_type.181), channel_id=1, source_target_pairs={{0,32},{8,40},{16,48},{24,56},{32,0},{40,8},{48,16},{56,24},{64,96... | collective-permute-start | bytes 73736 | tf_op jit(solution)/shard_map/ppermute | solution.py:43
  15.7 5.7 %collective-permute-start.2 = (bf16[48,256]{1,0:T(8,128)(2,1)S(1)}, bf16[48,256]{1,0:T(8,128)(2,1)S(1)}, u32[]{:S(2)}, u32[]{:S(2)}) collective-permute-start(bf16[48,256]{1,0:T(8,128)(2,1)S(1)} %convert_element_type.181), channel_id=1, source_target_pairs={{0,16},{8,24},{16,32},{24,40},{32,48},{40,56},{48,0},{56,8},{64,80... | collective-permute-start | bytes 73736 | tf_op jit(solution)/shard_map/ppermute | solution.py:43
  18.1 1.4 copy-start.2
  21.4 4.5 %collective-permute-start.3 = (bf16[192,256]{1,0:T(8,128)(2,1)S(1)}, bf16[192,256]{1,0:T(8,128)(2,1)S(1)}, u32[]{:S(2)}, u32[]{:S(2)}) collective-permute-start(bf16[192,256]{1,0:T(8,128)(2,1)S(1)} %fusion.29), channel_id=1, source_target_pairs={{0,192},{8,200},{16,208},{24,216},{32,224},{40,232},{48,240},{56,2... | collective-permute-start | bytes 294920 | tf_op jit(solution)/shard_map/ppermute | solution.py:39
  24.2 5.1 %collective-permute-start.4 = (bf16[192,256]{1,0:T(8,128)(2,1)S(1)}, bf16[192,256]{1,0:T(8,128)(2,1)S(1)}, u32[]{:S(2)}, u32[]{:S(2)}) collective-permute-start(bf16[192,256]{1,0:T(8,128)(2,1)S(1)} %fusion.29), channel_id=1, source_target_pairs={{0,128},{8,136},{16,144},{24,152},{32,160},{40,168},{48,176},{56,1... | collective-permute-start | bytes 294920 | tf_op jit(solution)/shard_map/ppermute | solution.py:39
  24.6 5.7 %collective-permute-start.5 = (bf16[192,256]{1,0:T(8,128)(2,1)S(1)}, bf16[192,256]{1,0:T(8,128)(2,1)S(1)}, u32[]{:S(2)}, u32[]{:S(2)}) collective-permute-start(bf16[192,256]{1,0:T(8,128)(2,1)S(1)} %fusion.29), channel_id=1, source_target_pairs={{0,64},{8,72},{16,80},{24,88},{32,96},{40,104},{48,112},{56,120},{... | collective-permute-start | bytes 294920 | tf_op jit(solution)/shard_map/ppermute | solution.py:39
  30.3 5.0 %copy-start.6 = (bf16[768,256]{1,0:T(8,128)(2,1)}, bf16[768,256]{1,0:T(8,128)(2,1)S(1)}, u32[]{:S(2)}) copy-start(bf16[768,256]{1,0:T(8,128)(2,1)S(1)} %get-tuple-element.58) | copy-start | bytes 1179652
  30.3 5.0 %collective-permute-start.6 = (bf16[768,256]{1,0:T(8,128)(2,1)S(1)}, bf16[768,256]{1,0:T(8,128)(2,1)S(1)}, u32[]{:S(2)}, u32[]{:S(2)}) collective-permute-start(bf16[768,256]{1,0:T(8,128)(2,1)S(1)} %get-tuple-element.58), channel_id=1, source_target_pairs={{0,8},{8,0},{16,24},{24,16},{32,40},{40,32},{48,56},{56,48},{64,72... | collective-permute-start | bytes 1179656 | tf_op jit(solution)/shard_map/ppermute | solution.py:47
  35.3 0.8 copy-start.3
  36.1 0.9 copy-start.5
  48.7 9.5 %all-to-all-start.1 = ((bf16[8,32,512]{2,1,0:T(8,128)(2,1)}), bf16[8,32,512]{2,1,0:T(8,128)(2,1)S(1)}, u32[]{:S(2)}, u32[]{:S(2)}) async-start(bf16[8,32,512]{2,1,0:T(8,128)(2,1)} %broadcast_in_dim.24), calls=%async_computation.1 | async-start | bytes 524288 | tf_op jit(solution)/shard_map/all_to_all | solution.py:105
  52.1 120.2 %all-gather.2.cloned.1.call-start = ((), (), s32[]{:S(2)}) async-start(), calls=%async_computation.4 | async-start | bytes 1892352 | tf_op jit(solution)/shard_map/all_gather | solution.py:266
  58.5 2.0 %copy-start = (bf16[512,3584]{1,0:T(8,128)(2,1)S(1)}, bf16[512,3584]{1,0:T(8,128)(2,1)}, u32[]{:S(2)}) copy-start(bf16[512,3584]{1,0:T(8,128)(2,1)} %cot_ref.1) | copy-start | bytes 11010052
  62.6 5.1 %collective-permute-start.7 = (bf16[128,3584]{1,0:T(8,128)(2,1)}, bf16[128,3584]{1,0:T(8,128)(2,1)}, u32[]{:S(2)}, u32[]{:S(2)}) collective-permute-start(bf16[128,3584]{1,0:T(8,128)(2,1)} %get-tuple-element.21), channel_id=1, source_target_pairs={{0,8},{8,0},{16,24},{24,16},{32,40},{40,32},{48,56},{56,48},{64,72... | collective-permute-start | bytes 2752520 | tf_op jit(solution)/shard_map/ppermute | solution.py:47
  69.1 5.5 %collective-permute-start.11 = (bf16[320,256]{1,0:T(8,128)(2,1)S(1)}, bf16[320,256]{1,0:T(8,128)(2,1)S(1)}, u32[]{:S(2)}, u32[]{:S(2)}) collective-permute-start(bf16[320,256]{1,0:T(8,128)(2,1)S(1)} %pad_maximum_fusion.6), channel_id=1, source_target_pairs={{0,1},{1,0},{2,3},{3,2},{4,5},{5,4},{6,7},{7,6},{8,9},{9,8},{10,11... | collective-permute-start | bytes 491528 | tf_op jit(solution)/shard_map/ppermute | solution.py:51
  69.8 6.6 %collective-permute-start.10 = (bf16[32,3584]{1,0:T(8,128)(2,1)S(1)}, bf16[32,3584]{1,0:T(8,128)(2,1)S(1)}, u32[]{:S(2)}, u32[]{:S(2)}) collective-permute-start(bf16[32,3584]{1,0:T(8,128)(2,1)S(1)} %get-tuple-element.45), channel_id=1, source_target_pairs={{0,192},{8,200},{16,208},{24,216},{32,224},{40,232},{48,240},{56,2... | collective-permute-start | bytes 688136 | tf_op jit(solution)/shard_map/ppermute | solution.py:39
  70.1 7.7 %collective-permute-start.8 = (bf16[32,3584]{1,0:T(8,128)(2,1)S(1)}, bf16[32,3584]{1,0:T(8,128)(2,1)S(1)}, u32[]{:S(2)}, u32[]{:S(2)}) collective-permute-start(bf16[32,3584]{1,0:T(8,128)(2,1)S(1)} %get-tuple-element.44), channel_id=1, source_target_pairs={{0,128},{8,136},{16,144},{24,152},{32,160},{40,168},{48,176},{56,1... | collective-permute-start | bytes 688136 | tf_op jit(solution)/shard_map/ppermute | solution.py:39
  70.6 13.4 %collective-permute-start.9 = (bf16[32,3584]{1,0:T(8,128)(2,1)S(1)}, bf16[32,3584]{1,0:T(8,128)(2,1)S(1)}, u32[]{:S(2)}, u32[]{:S(2)}) collective-permute-start(bf16[32,3584]{1,0:T(8,128)(2,1)S(1)} %get-tuple-element.46), channel_id=1, source_target_pairs={{0,64},{8,72},{16,80},{24,88},{32,96},{40,104},{48,112},{56,120},{... | collective-permute-start | bytes 688136 | tf_op jit(solution)/shard_map/ppermute | solution.py:39
  74.7 20.6 %copy-start.8 = (f32[8,3584]{1,0:T(8,128)S(1)}, f32[8,3584]{1,0:T(8,128)}, u32[]{:S(2)}) copy-start(f32[8,3584]{1,0:T(8,128)} %param.10) | copy-start | bytes 344068
  74.7 20.6 %copy-start.9 = (f32[8,3584]{1,0:T(8,128)S(1)}, f32[8,3584]{1,0:T(8,128)}, u32[]{:S(2)}) copy-start(f32[8,3584]{1,0:T(8,128)} %param.11) | copy-start | bytes 344068
  74.7 9.5 %collective-permute-start.12 = (bf16[368,256]{1,0:T(8,128)(2,1)S(1)}, bf16[368,256]{1,0:T(8,128)(2,1)S(1)}, u32[]{:S(2)}, u32[]{:S(2)}) collective-permute-start(bf16[368,256]{1,0:T(8,128)(2,1)S(1)} %pad_maximum_fusion.5), channel_id=1, source_target_pairs={{0,2},{1,3},{2,0},{3,1},{4,6},{5,7},{6,4},{7,5},{8,10},{9,11},{10,... | collective-permute-start | bytes 565256 | tf_op jit(solution)/shard_map/ppermute | solution.py:51
  84.4 7.7 %collective-permute-start.13 = (bf16[8,3584]{1,0:T(8,128)(2,1)S(1)}, bf16[8,3584]{1,0:T(8,128)(2,1)S(1)}, u32[]{:S(2)}, u32[]{:S(2)}) collective-permute-start(bf16[8,3584]{1,0:T(8,128)(2,1)S(1)} %get-tuple-element.52), channel_id=1, source_target_pairs={{0,32},{8,40},{16,48},{24,56},{32,0},{40,8},{48,16},{56,24},{64,96... | collective-permute-start | bytes 172040 | tf_op jit(solution)/shard_map/ppermute | solution.py:43
  88.5 5.5 %collective-permute-start.14 = (bf16[8,3584]{1,0:T(8,128)(2,1)S(1)}, bf16[8,3584]{1,0:T(8,128)(2,1)S(1)}, u32[]{:S(2)}, u32[]{:S(2)}) collective-permute-start(bf16[8,3584]{1,0:T(8,128)(2,1)S(1)} %get-tuple-element.54), channel_id=1, source_target_pairs={{0,16},{8,24},{16,32},{24,40},{32,48},{40,56},{48,0},{56,8},{64,80... | collective-permute-start | bytes 172040 | tf_op jit(solution)/shard_map/ppermute | solution.py:43
  88.5 6.8 %collective-permute-start.15 = (bf16[8,3584]{1,0:T(8,128)(2,1)S(1)}, bf16[8,3584]{1,0:T(8,128)(2,1)S(1)}, u32[]{:S(2)}, u32[]{:S(2)}) collective-permute-start(bf16[8,3584]{1,0:T(8,128)(2,1)S(1)} %get-tuple-element.53), channel_id=1, source_target_pairs={{0,48},{8,56},{16,0},{24,8},{32,16},{40,24},{48,32},{56,40},{64,11... | collective-permute-start | bytes 172040 | tf_op jit(solution)/shard_map/ppermute | solution.py:43
  96.1 7.0 %collective-permute-start.16 = (bf16[8,3584]{1,0:T(8,128)(2,1)S(1)}, bf16[8,3584]{1,0:T(8,128)(2,1)S(1)}, u32[]{:S(2)}, u32[]{:S(2)}) collective-permute-start(bf16[8,3584]{1,0:T(8,128)(2,1)S(1)} %get-tuple-element.37), channel_id=1, source_target_pairs={{0,48},{8,56},{16,0},{24,8},{32,16},{40,24},{48,32},{56,40},{64,11... | collective-permute-start | bytes 172040 | tf_op jit(solution)/shard_map/ppermute | solution.py:43
  98.0 7.1 %collective-permute-start.17 = (bf16[8,3584]{1,0:T(8,128)(2,1)S(1)}, bf16[8,3584]{1,0:T(8,128)(2,1)S(1)}, u32[]{:S(2)}, u32[]{:S(2)}) collective-permute-start(bf16[8,3584]{1,0:T(8,128)(2,1)S(1)} %get-tuple-element.37), channel_id=1, source_target_pairs={{0,32},{8,40},{16,48},{24,56},{32,0},{40,8},{48,16},{56,24},{64,96... | collective-permute-start | bytes 172040 | tf_op jit(solution)/shard_map/ppermute | solution.py:43
  99.8 7.0 %collective-permute-start.18 = (bf16[8,3584]{1,0:T(8,128)(2,1)S(1)}, bf16[8,3584]{1,0:T(8,128)(2,1)S(1)}, u32[]{:S(2)}, u32[]{:S(2)}) collective-permute-start(bf16[8,3584]{1,0:T(8,128)(2,1)S(1)} %get-tuple-element.37), channel_id=1, source_target_pairs={{0,16},{8,24},{16,32},{24,40},{32,48},{40,56},{48,0},{56,8},{64,80... | collective-permute-start | bytes 172040 | tf_op jit(solution)/shard_map/ppermute | solution.py:43
  101.7 6.8 %collective-permute-start.19 = (bf16[464,256]{1,0:T(8,128)(2,1)S(1)}, bf16[464,256]{1,0:T(8,128)(2,1)S(1)}, u32[]{:S(2)}, u32[]{:S(2)}) collective-permute-start(bf16[464,256]{1,0:T(8,128)(2,1)S(1)} %pad_maximum_fusion.2), channel_id=1, source_target_pairs={{0,6},{1,7},{2,4},{3,5},{4,2},{5,3},{6,0},{7,1},{8,14},{9,15},{10,... | collective-permute-start | bytes 712712 | tf_op jit(solution)/shard_map/ppermute | solution.py:51
  108.7 4.9 %collective-permute-start.20 = (bf16[32,3584]{1,0:T(8,128)(2,1)S(1)}, bf16[32,3584]{1,0:T(8,128)(2,1)S(1)}, u32[]{:S(2)}, u32[]{:S(2)}) collective-permute-start(bf16[32,3584]{1,0:T(8,128)(2,1)S(1)} %pad_maximum_fusion.3), channel_id=1, source_target_pairs={{0,192},{8,200},{16,208},{24,216},{32,224},{40,232},{48,240},{56,2... | collective-permute-start | bytes 688136 | tf_op jit(solution)/shard_map/ppermute | solution.py:39
  108.8 6.6 %collective-permute-start.21 = (bf16[32,3584]{1,0:T(8,128)(2,1)S(1)}, bf16[32,3584]{1,0:T(8,128)(2,1)S(1)}, u32[]{:S(2)}, u32[]{:S(2)}) collective-permute-start(bf16[32,3584]{1,0:T(8,128)(2,1)S(1)} %pad_maximum_fusion.3), channel_id=1, source_target_pairs={{0,128},{8,136},{16,144},{24,152},{32,160},{40,168},{48,176},{56,1... | collective-permute-start | bytes 688136 | tf_op jit(solution)/shard_map/ppermute | solution.py:39
  109.4 12.6 %collective-permute-start.22 = (bf16[32,3584]{1,0:T(8,128)(2,1)S(1)}, bf16[32,3584]{1,0:T(8,128)(2,1)S(1)}, u32[]{:S(2)}, u32[]{:S(2)}) collective-permute-start(bf16[32,3584]{1,0:T(8,128)(2,1)S(1)} %pad_maximum_fusion.3), channel_id=1, source_target_pairs={{0,64},{8,72},{16,80},{24,88},{32,96},{40,104},{48,112},{56,120},{... | collective-permute-start | bytes 688136 | tf_op jit(solution)/shard_map/ppermute | solution.py:39
  122.0 4.2 %copy-start.1 = (bf16[512,3584]{1,0:T(8,128)(2,1)S(1)}, bf16[512,3584]{1,0:T(8,128)(2,1)}, u32[]{:S(2)}) copy-start(bf16[512,3584]{1,0:T(8,128)(2,1)} %cot_ref.1) | copy-start | bytes 11010052
  122.1 4.0 %collective-permute-start.23 = (bf16[128,3584]{1,0:T(8,128)(2,1)S(1)}, bf16[128,3584]{1,0:T(8,128)(2,1)S(1)}, u32[]{:S(2)}, u32[]{:S(2)}) collective-permute-start(bf16[128,3584]{1,0:T(8,128)(2,1)S(1)} %pad_maximum_fusion), channel_id=1, source_target_pairs={{0,8},{8,0},{16,24},{24,16},{32,40},{40,32},{48,56},{56,48},{64,72... | collective-permute-start | bytes 2752520 | tf_op jit(solution)/shard_map/ppermute | solution.py:47
  128.7 11.6 %all-to-all-start.2 = ((bf16[8,48,512]{2,1,0:T(8,128)(2,1)}), bf16[8,48,512]{2,1,0:T(8,128)(2,1)S(1)}, u32[]{:S(2)}, u32[]{:S(2)}) async-start(bf16[8,48,512]{2,1,0:T(8,128)(2,1)} %pad_maximum_fusion.1), calls=%async_computation.2 | async-start | bytes 786432 | tf_op jit(solution)/shard_map/all_to_all | solution.py:94
  141.1 13.1 %all-to-all-start.3 = ((bf16[8,32,512]{2,1,0:T(8,128)(2,1)}), bf16[8,32,512]{2,1,0:T(8,128)(2,1)S(1)}, u32[]{:S(2)}, u32[]{:S(2)}) async-start(bf16[8,32,512]{2,1,0:T(8,128)(2,1)} %broadcast_in_dim.29), calls=%async_computation.3 | async-start | bytes 524288 | tf_op jit(solution)/shard_map/all_to_all | solution.py:105
  144.7 10.2 %copy-start.4 = (bf16[768,256]{1,0:T(8,128)(2,1)S(1)}, bf16[768,256]{1,0:T(8,128)(2,1)}, u32[]{:S(2)}) copy-start(bf16[768,256]{1,0:T(8,128)(2,1)} %copy-done.3) | copy-start | bytes 1179652
  154.9 3.1 %copy-start.7 = (bf16[768,256]{1,0:T(8,128)(2,1)S(1)}, bf16[768,256]{1,0:T(8,128)(2,1)}, u32[]{:S(2)}) copy-start(bf16[768,256]{1,0:T(8,128)(2,1)} %copy-done.6) | copy-start | bytes 1179652
  155.2 2.8 %collective-permute-start.24 = (bf16[768,256]{1,0:T(8,128)(2,1)S(1)}, bf16[768,256]{1,0:T(8,128)(2,1)S(1)}, u32[]{:S(2)}, u32[]{:S(2)}) collective-permute-start(bf16[768,256]{1,0:T(8,128)(2,1)S(1)} %fusion.1), channel_id=1, source_target_pairs={{0,8},{8,0},{16,24},{24,16},{32,40},{40,32},{48,56},{56,48},{64,72... | collective-permute-start | bytes 1179656 | tf_op jit(solution)/shard_map/ppermute | solution.py:47
  158.3 5.6 %collective-permute-start.25 = (bf16[192,256]{1,0:T(8,128)(2,1)S(1)}, bf16[192,256]{1,0:T(8,128)(2,1)S(1)}, u32[]{:S(2)}, u32[]{:S(2)}) collective-permute-start(bf16[192,256]{1,0:T(8,128)(2,1)S(1)} %get-tuple-element.49), channel_id=1, source_target_pairs={{0,128},{8,136},{16,144},{24,152},{32,160},{40,168},{48,176},{56,1... | collective-permute-start | bytes 294920 | tf_op jit(solution)/shard_map/ppermute | solution.py:39
  160.0 6.3 %collective-permute-start.26 = (bf16[192,256]{1,0:T(8,128)(2,1)S(1)}, bf16[192,256]{1,0:T(8,128)(2,1)S(1)}, u32[]{:S(2)}, u32[]{:S(2)}) collective-permute-start(bf16[192,256]{1,0:T(8,128)(2,1)S(1)} %get-tuple-element.51), channel_id=1, source_target_pairs={{0,64},{8,72},{16,80},{24,88},{32,96},{40,104},{48,112},{56,120},{... | collective-permute-start | bytes 294920 | tf_op jit(solution)/shard_map/ppermute | solution.py:39
  160.7 5.6 %collective-permute-start.27 = (bf16[192,256]{1,0:T(8,128)(2,1)S(1)}, bf16[192,256]{1,0:T(8,128)(2,1)S(1)}, u32[]{:S(2)}, u32[]{:S(2)}) collective-permute-start(bf16[192,256]{1,0:T(8,128)(2,1)S(1)} %get-tuple-element.50), channel_id=1, source_target_pairs={{0,192},{8,200},{16,208},{24,216},{32,224},{40,232},{48,240},{56,2... | collective-permute-start | bytes 294920 | tf_op jit(solution)/shard_map/ppermute | solution.py:39
  166.4 11.0 %collective-permute-start.28 = (bf16[48,256]{1,0:T(8,128)(2,1)S(1)}, bf16[48,256]{1,0:T(8,128)(2,1)S(1)}, u32[]{:S(2)}, u32[]{:S(2)}) collective-permute-start(bf16[48,256]{1,0:T(8,128)(2,1)S(1)} %get-tuple-element.55), channel_id=1, source_target_pairs={{0,32},{8,40},{16,48},{24,56},{32,0},{40,8},{48,16},{56,24},{64,96... | collective-permute-start | bytes 73736 | tf_op jit(solution)/shard_map/ppermute | solution.py:43
  168.7 8.6 %collective-permute-start.29 = (bf16[48,256]{1,0:T(8,128)(2,1)S(1)}, bf16[48,256]{1,0:T(8,128)(2,1)S(1)}, u32[]{:S(2)}, u32[]{:S(2)}) collective-permute-start(bf16[48,256]{1,0:T(8,128)(2,1)S(1)} %get-tuple-element.57), channel_id=1, source_target_pairs={{0,16},{8,24},{16,32},{24,40},{32,48},{40,56},{48,0},{56,8},{64,80... | collective-permute-start | bytes 73736 | tf_op jit(solution)/shard_map/ppermute | solution.py:43
  169.9 7.4 %collective-permute-start.30 = (bf16[48,256]{1,0:T(8,128)(2,1)S(1)}, bf16[48,256]{1,0:T(8,128)(2,1)S(1)}, u32[]{:S(2)}, u32[]{:S(2)}) collective-permute-start(bf16[48,256]{1,0:T(8,128)(2,1)S(1)} %get-tuple-element.56), channel_id=1, source_target_pairs={{0,48},{8,56},{16,0},{24,8},{32,16},{40,24},{48,32},{56,40},{64,11... | collective-permute-start | bytes 73736 | tf_op jit(solution)/shard_map/ppermute | solution.py:43
Sparse Core Ops, SparseCore 0:
  103.2 52.7 all-gather.1
